TPU v7x, 256 devices: a whole 4x4x8 slice. The times are simulated.
256 devices in a mesh: dp: 16 (over z_lo, y), et: 16 (over z_hi, x, core).
Axes of the slice: x: 4, y: 4, z: 8 (z_hi: 2, z_lo: 4; z = z_hi * 4 + z_lo), core: 2. Of those that a mesh axis runs over, the one named last changes fastest.
Arguments:
- tokens: bfloat16 [2048, 4096], P('dp'), may hold values from -6 to 6
- expert_ids: int32 [2048, 2], P('dp'), may hold values from 0 to 7, as said below
- gate_fixed: int32 [2048, 2], P('dp'), may hold values from 1 to 32767
- w_gate: bfloat16 [2, 4096, 14336], P(None, 'dp', 'et'), may hold values from -0.09375 to 0.09375
- w_up: bfloat16 [2, 4096, 14336], P(None, 'dp', 'et'), may hold values from -0.09375 to 0.09375
- w_down: bfloat16 [2, 14336, 4096], P(None, 'et', 'dp'), may hold values from -0.046875 to 0.046875
- d_out: bfloat16 [2048, 4096], P('dp'), may hold values from -6 to 6
Outputs:
- mixed: float32 [2048, 4096], P('dp', 'et')
- grad_tokens: float32 [2048, 4096], P('dp', 'et')
- grad_gate: float32 [2, 4096, 14336], P(None, 'dp', 'et')
- grad_up: float32 [2, 4096, 14336], P(None, 'dp', 'et')
- grad_down: float32 [2, 14336, 4096], P(None, 'et', 'dp')
Inputs may be any that keep to these rules, and one draw needn't show every extreme that they name: `expert_ids`: each row names two different experts. Among the 128 tokens of one index of dp, at most 32 name any one expert below 2, and for each such expert some index reaches 32 in every draw.
All inputs are finite; a program needn't handle non-finite values.
Results may differ from a plain program's by a relative error of at most 0.0041.
Values may be sent and summed in bfloat16 or wider, within the bound.
No kernel may reach another device: no remote copies, remote signals or barrier semaphores. Data moves between devices by JAX's collectives and lax.ppermute only.
A program may use at most 64 MiB of HBM per device.

v0:
```python
import jax
import jax.numpy as jnp
from jax import lax
from jax.sharding import PartitionSpec as P

CAP = 32


def route_table(expert_ids, gate_fixed, experts, capacity):
    expert_range = jnp.arange(experts, dtype=jnp.int32)
    picked = (expert_ids[None, :, :] == expert_range[:, None, None]).astype(jnp.int32)
    member = jnp.sum(picked, axis=2)
    scaled = jnp.sum(picked * gate_fixed[None, :, :], axis=2).astype(jnp.float32) / 32768.0
    before = jnp.cumsum(member, axis=1) - member
    slot_range = jnp.arange(capacity, dtype=jnp.int32)
    hit = (member[:, None, :] == 1) & (before[:, None, :] == slot_range[None, :, None])
    dispatch = hit.astype(jnp.float32)
    row_weight = jnp.sum(dispatch * scaled[:, None, :], axis=2)
    return (dispatch, row_weight)


def sum_features(terms, rows):
    return lax.psum_scatter(
        terms(jnp.int32(0), rows * lax.axis_size("dp")), "dp", scatter_dimension=0, tiled=True
    )


def gather_rows(values):
    return lax.all_gather(values, "dp", axis=0, tiled=True)


def to_group_rows(values):
    return lax.all_to_all(values, "dp", split_axis=0, concat_axis=1, tiled=True)


def sum_units(values):
    return lax.psum_scatter(values, "et", scatter_dimension=1, tiled=True)


def expert_pass(routed, d_rows, w_gate, w_up, w_down, lower, upper):
    span = upper - lower
    rows = span * CAP
    width_block = w_gate.shape[1]
    unit_width = w_gate.shape[2]
    routed_all, grads_all = (
        lax.all_to_all(routed, "dp", split_axis=1, concat_axis=0, tiled=True),
        lax.all_to_all(d_rows, "dp", split_axis=1, concat_axis=0, tiled=True),
    )

    def gate_terms(start, length):
        block_rows = routed_all.reshape(length // rows, span, CAP, width_block)
        gate_part = jnp.einsum(
            "gkcd,kdf->gkcf", block_rows, w_gate, preferred_element_type=jnp.float32
        )
        up_part = jnp.einsum("gkcd,kdf->gkcf", block_rows, w_up, preferred_element_type=jnp.float32)
        return jnp.concatenate([gate_part, up_part], axis=3).reshape(length, 2 * unit_width)

    summed = sum_features(gate_terms, rows)
    gate = summed[:, :unit_width]
    up = summed[:, unit_width:]
    sigma = jax.nn.sigmoid(gate)
    hidden = (gate * sigma * up).astype(jnp.bfloat16)
    hidden_all = gather_rows(hidden)
    groups_hidden = hidden_all.reshape(-1, span, CAP, unit_width)
    down_part = jnp.einsum(
        "gkcf,kfd->gkcd", groups_hidden, w_down, preferred_element_type=jnp.float32
    )
    down_rows = to_group_rows(down_part.reshape(-1, width_block))
    groups_grads = grads_all.reshape(-1, span, CAP, width_block)
    grad_down = jnp.einsum(
        "gkcf,gkcd->kfd", groups_hidden, groups_grads, preferred_element_type=jnp.float32
    )

    def hidden_terms(start, length):
        block_rows = grads_all.reshape(length // rows, span, CAP, width_block)
        part = jnp.einsum("gkcd,kfd->gkcf", block_rows, w_down, preferred_element_type=jnp.float32)
        return part.reshape(length, unit_width)

    d_hidden = sum_features(hidden_terms, rows)
    d_gate = (d_hidden * up * sigma * (1.0 + gate * (1.0 - sigma))).astype(jnp.bfloat16)
    d_up = (d_hidden * gate * sigma).astype(jnp.bfloat16)
    both_all = gather_rows(jnp.concatenate([d_gate, d_up], axis=1))
    groups_both = both_all.reshape(-1, span, CAP, 2 * unit_width)
    groups_routed = routed_all.reshape(-1, span, CAP, width_block)
    grad_both = jnp.einsum(
        "gkcd,gkcf->kdf", groups_routed, groups_both, preferred_element_type=jnp.float32
    )
    back_part = jnp.einsum(
        "gkcf,kdf->gkcd", groups_both[..., :unit_width], w_gate, preferred_element_type=jnp.float32
    )
    back_part = back_part + jnp.einsum(
        "gkcf,kdf->gkcd", groups_both[..., unit_width:], w_up, preferred_element_type=jnp.float32
    )
    d_routed = to_group_rows(back_part.reshape(-1, width_block))
    return (
        down_rows,
        d_routed,
        grad_both[:, :, :unit_width],
        grad_both[:, :, unit_width:],
        grad_down,
    )


def local(tokens, expert_ids, gate_fixed, w_gate, w_up, w_down, d_out):
    highest = lax.Precision.HIGHEST
    experts = w_gate.shape[0]
    token_rows = tokens.shape[0]
    dispatch, row_weight = route_table(expert_ids, gate_fixed, experts, CAP)
    flat_dispatch = dispatch.reshape(experts * CAP, token_rows)
    flat_weight = row_weight.reshape(experts * CAP)
    send_dispatch = flat_dispatch.astype(jnp.bfloat16)
    routed = jnp.dot(send_dispatch, tokens, preferred_element_type=jnp.float32).astype(jnp.bfloat16)
    d_rows = (
        flat_weight[:, None] * jnp.dot(send_dispatch, d_out, preferred_element_type=jnp.float32)
    ).astype(jnp.bfloat16)
    spans = [(0, experts)]
    results = [
        expert_pass(routed, d_rows, w_gate, w_up, w_down, lower, upper) for lower, upper in spans
    ]
    down_rows = jnp.concatenate([item[0] for item in results], axis=0)
    d_routed = jnp.concatenate([item[1] for item in results], axis=0)
    grad_gate = jnp.concatenate([item[2] for item in results], axis=0)
    grad_up = jnp.concatenate([item[3] for item in results], axis=0)
    grad_down = jnp.concatenate([item[4] for item in results], axis=0)
    weighted = flat_dispatch * flat_weight[:, None]
    first_terms = jnp.einsum("rt,rd->td", weighted, down_rows, precision=highest)
    second_terms = jnp.einsum("rt,rd->td", flat_dispatch, d_routed, precision=highest)
    first_sum = sum_units(first_terms)
    second_sum = sum_units(second_terms)
    return (first_sum, second_sum, grad_gate, grad_up, grad_down)


def solution(mesh):
    placed = (
        P("dp", None),
        P("dp", None),
        P("dp", None),
        P(None, "dp", "et"),
        P(None, "dp", "et"),
        P(None, "et", "dp"),
        P("dp", None),
    )
    return jax.shard_map(
        local,
        mesh=mesh,
        in_specs=placed,
        out_specs=(
            P("dp", "et"),
            P("dp", "et"),
            P(None, "dp", "et"),
            P(None, "dp", "et"),
            P(None, "et", "dp"),
        ),
        check_vma=False,
    )
```

profile of v0, /device:TPU:67, one launch (start us, length us, event | category | flops | bytes accessed | tf_op | source)
XLA Modules:
  0.0 581.0 jit_solution(6095693036463896583)
XLA Ops:
  7.2 0.0 copy-start
  7.2 0.0 copy-start.5
  7.2 0.0 reduce-scatter.9.cloned.1.call-start
  7.2 0.8 convert_reduce_fusion
  8.1 0.3 reduce_window_sum.11
  8.4 0.1 eq.73
  8.5 0.1 convert_convert_fusion
  8.6 0.1 select_reduce_fusion
  8.7 0.1 mul.70
  8.8 0.0 copy-done
  8.8 0.3 fusion
  9.1 22.0 %all_to_all.70 = bf16[64,16,256]{2,0,1:T(8,128)(2,1)S(1)} all-to-all(bf16[64,16,256]{2,0,1:T(8,128)(2,1)S(1)} %bitcast.98), channel_id=1, replica_groups=mesh['dp'=16,'et'=16] {'dp'}, dimensions={1} | all-to-all | bytes 1048576 | tf_op jit(solution)/shard_map/all_to_all | solution.py:47
  31.1 0.0 copy-done.5
  31.1 0.7 convolution_bitcast_fusion.1
  31.9 2.2 copy.43
  34.1 0.0 reduce-scatter.9.cloned.1.call-update
  34.1 0.0 reduce-scatter.5.cloned.1.call-start
  34.2 1.1 copy-done.4
  35.3 0.3 convolution_convert_fusion
  35.7 18.5 %all_to_all.71 = bf16[64,16,256]{2,0,1:T(8,128)(2,1)S(1)} all-to-all(bf16[64,16,256]{2,0,1:T(8,128)(2,1)S(1)} %bitcast.99), channel_id=1, replica_groups=mesh['dp'=16,'et'=16] {'dp'}, dimensions={1} | all-to-all | bytes 1048576 | tf_op jit(solution)/shard_map/all_to_all | solution.py:46
  54.2 0.0 copy-done.7
  54.2 0.7 convolution_bitcast_fusion.2
  54.9 0.5 copy-done.3
  55.4 0.7 convolution_bitcast_fusion.3
  56.1 0.6 pad_maximum_fusion
  56.7 3.8 copy.37
  60.5 0.0 reduce-scatter.5.cloned.1.call-update
  60.5 0.0 all-gather.3.cloned.1.call-start
  60.6 45.1 %reduce-scatter.9.cloned.1.call-done = f32[64,896]{1,0:T(8,128)} async-done(((f32[1024,896]{1,0:T(8,128)}), f32[64,896]{1,0:T(8,128)}) %reduce-scatter.9.cloned.1.call-update) | async-done | bytes 229392 | tf_op jit(solution)/shard_map/reduce_scatter | solution.py:23
  105.7 107.7 %reduce-scatter.5.cloned.1.call-done = f32[64,1792]{1,0:T(8,128)} async-done(((f32[1024,1792]{1,0:T(8,128)}), f32[64,1792]{1,0:T(8,128)}) %reduce-scatter.5.cloned.1.call-update) | async-done | bytes 458768 | tf_op jit(solution)/shard_map/reduce_scatter | solution.py:23
  213.4 1.9 multiply_convert_fusion.1
  215.4 0.0 all-gather.3.cloned.1.call-update
  215.4 0.0 all-gather.5.cloned.1.call-start
  215.4 0.7 pad_maximum_fusion.1
  216.1 0.0 all-gather.5.cloned.1.call-update
  216.2 78.1 %all-gather.3.cloned.1.call-done = bf16[1024,896]{1,0:T(8,128)(2,1)} async-done(((bf16[64,896]{1,0:T(8,128)(2,1)}), bf16[1024,896]{1,0:T(8,128)(2,1)}) %all-gather.3.cloned.1.call-update) | async-done | bytes 1835024 | tf_op jit(solution)/shard_map/all_gather | solution.py:29
  294.3 0.0 copy-done.6
  294.3 2.2 fusion.7
  296.5 1.0 copy.39
  297.6 14.1 %all-to-all-start.1 = ((f32[16,64,256]{2,1,0:T(8,128)}), f32[16,64,256]{2,1,0:T(8,128)S(1)}, u32[]{:S(2)}, u32[]{:S(2)}) async-start(f32[16,64,256]{2,1,0:T(8,128)} %bitcast.17), calls=%async_computation.2 | async-start | bytes 2097152 | tf_op jit(solution)/shard_map/all_to_all | solution.py:33
  311.7 0.0 reduce-scatter.7.cloned.1.call-start
  311.7 0.1 broadcast_select_fusion
  311.8 15.1 %all-to-all-done.1 = f32[16,64,256]{2,1,0:T(8,128)S(1)} async-done(((f32[16,64,256]{2,1,0:T(8,128)}), f32[16,64,256]{2,1,0:T(8,128)S(1)}, u32[]{:S(2)}, u32[]{:S(2)}) %all-to-all-start.1) | async-done | bytes 1048608 | tf_op jit(solution)/shard_map/all_to_all | solution.py:33
  326.9 0.1 copy.55
  327.0 3.2 fusion.29
  330.2 0.0 reduce-scatter.7.cloned.1.call-update
  330.2 54.8 %all-gather.5.cloned.1.call-done = bf16[1024,1792]{1,0:T(8,128)(2,1)} async-done(((bf16[64,1792]{1,0:T(8,128)(2,1)}), bf16[1024,1792]{1,0:T(8,128)(2,1)}) %all-gather.5.cloned.1.call-update) | async-done | bytes 3670032 | tf_op jit(solution)/shard_map/all_gather | solution.py:29
  385.0 2.4 fusion.28
  387.4 0.0 copy-done.8
  387.4 0.7 fusion.1
  388.2 0.7 fusion.13
  388.9 1.1 copy.46
  390.0 13.4 %all-to-all-start.3 = ((f32[16,64,256]{2,1,0:T(8,128)}), f32[16,64,256]{2,1,0:T(8,128)S(1)}, u32[]{:S(2)}, u32[]{:S(2)}) async-start(f32[16,64,256]{2,1,0:T(8,128)} %bitcast.29), calls=%async_computation.6 | async-start | bytes 2097152 | tf_op jit(solution)/shard_map/all_to_all | solution.py:33
  403.4 0.2 reduce-scatter.11.cloned.1.call-start
  403.6 21.9 %all-to-all-done.3 = f32[16,64,256]{2,1,0:T(8,128)S(1)} async-done(((f32[16,64,256]{2,1,0:T(8,128)}), f32[16,64,256]{2,1,0:T(8,128)S(1)}, u32[]{:S(2)}, u32[]{:S(2)}) %all-to-all-start.3) | async-done | bytes 1048608 | tf_op jit(solution)/shard_map/all_to_all | solution.py:33
  425.6 0.1 copy.56
  425.7 2.4 fusion.30
  428.0 0.0 reduce-scatter.11.cloned.1.call-update
  428.1 3.7 convolution_bitcast_fusion.4
  431.8 0.0 copy-done.2
  431.8 1.2 convolution_bitcast_fusion
  433.0 2.1 fusion.27
  435.1 50.9 %reduce-scatter.7.cloned.1.call-done = f32[128,256]{1,0:T(8,128)} async-done(((f32[128,4096]{1,0:T(8,128)}), f32[128,256]{1,0:T(8,128)}) %reduce-scatter.7.cloned.1.call-update) | async-done | bytes 131088 | tf_op jit(solution)/shard_map/reduce_scatter | solution.py:37
  486.0 88.2 %reduce-scatter.11.cloned.1.call-done = f32[128,256]{1,0:T(8,128)} async-done(((f32[128,4096]{1,0:T(8,128)}), f32[128,256]{1,0:T(8,128)}) %reduce-scatter.11.cloned.1.call-update) | async-done | bytes 131088 | tf_op jit(solution)/shard_map/reduce_scatter | solution.py:37
  (15 shorter events, 0.1 us)
Async XLA Ops:
  7.2 1.6 copy-start
  7.2 23.9 %copy-start.5 = (bf16[2,896,256]{2,1,0:T(8,128)(2,1)S(1)}, bf16[2,896,256]{2,1,0:T(8,128)(2,1)}, u32[]{:S(2)}) copy-start(bf16[2,896,256]{2,1,0:T(8,128)(2,1)} %param.12) | copy-start | bytes 2752516
  7.2 98.5 %reduce-scatter.9.cloned.1.call-start = ((), (), s32[]{:S(2)}) async-start(), calls=%async_computation.11 | async-start | bytes 3899392 | tf_op jit(solution)/shard_map/reduce_scatter | solution.py:23
  34.1 1.2 copy-start.4
  34.1 179.3 %reduce-scatter.5.cloned.1.call-start = ((), (), s32[]{:S(2)}) async-start(), calls=%async_computation.8 | async-start | bytes 7798784 | tf_op jit(solution)/shard_map/reduce_scatter | solution.py:23
  35.3 18.9 %copy-start.7 = (bf16[2,256,896]{2,1,0:T(8,128)(2,1)S(1)}, bf16[2,256,896]{2,1,0:T(8,128)(2,1)}, u32[]{:S(2)}) copy-start(bf16[2,256,896]{2,1,0:T(8,128)(2,1)} %param.11) | copy-start | bytes 2752516
  54.2 1.2 copy-start.3
  60.5 233.8 %copy-start.6 = (bf16[2,896,256]{2,1,0:T(8,128)(2,1)S(1)}, bf16[2,896,256]{2,1,0:T(8,128)(2,1)}, u32[]{:S(2)}) copy-start(bf16[2,896,256]{2,1,0:T(8,128)(2,1)} %param.12) | copy-start | bytes 2752516
  60.5 233.8 %all-gather.3.cloned.1.call-start = ((), (), s32[]{:S(2)}) async-start(), calls=%async_computation.9 | async-start | bytes 1949696 | tf_op jit(solution)/shard_map/all_gather | solution.py:29
  215.4 169.6 %all-gather.5.cloned.1.call-start = ((), (), s32[]{:S(2)}) async-start(), calls=%async_computation.12 | async-start | bytes 3899392 | tf_op jit(solution)/shard_map/all_gather | solution.py:29
  297.6 29.3 %all-to-all-start.1 = ((f32[16,64,256]{2,1,0:T(8,128)}), f32[16,64,256]{2,1,0:T(8,128)S(1)}, u32[]{:S(2)}, u32[]{:S(2)}) async-start(f32[16,64,256]{2,1,0:T(8,128)} %bitcast.17), calls=%async_computation.2 | async-start | bytes 2097152 | tf_op jit(solution)/shard_map/all_to_all | solution.py:33
  311.7 174.3 %reduce-scatter.7.cloned.1.call-start = ((), (), s32[]{:S(2)}) async-start(), calls=%async_computation.10 | async-start | bytes 2228224 | tf_op jit(solution)/shard_map/reduce_scatter | solution.py:37
  385.0 2.5 copy-start.8
  390.0 35.6 %all-to-all-start.3 = ((f32[16,64,256]{2,1,0:T(8,128)}), f32[16,64,256]{2,1,0:T(8,128)S(1)}, u32[]{:S(2)}, u32[]{:S(2)}) async-start(f32[16,64,256]{2,1,0:T(8,128)} %bitcast.29), calls=%async_computation.6 | async-start | bytes 2097152 | tf_op jit(solution)/shard_map/all_to_all | solution.py:33
  403.4 170.8 %reduce-scatter.11.cloned.1.call-start = ((), (), s32[]{:S(2)}) async-start(), calls=%async_computation.13 | async-start | bytes 2228224 | tf_op jit(solution)/shard_map/reduce_scatter | solution.py:37
  428.1 3.7 copy-start.2
  431.8 142.4 %copy-start.1 = (bf16[128,4096]{1,0:T(8,128)(2,1)S(1)}, bf16[128,4096]{1,0:T(8,128)(2,1)}, u32[]{:S(2)}) copy-start(bf16[128,4096]{1,0:T(8,128)(2,1)} %param.13) | copy-start | bytes 3145732
Sparse Core Ops, SparseCore 0:
  34.3 71.3 reduce-scatter.8
  108.3 105.1 reduce-scatter.4
  215.8 78.4 all-gather.2
  296.5 88.3 all-gather.4
  389.6 96.3 reduce-scatter.6
  490.7 83.4 reduce-scatter.10
where the time goes:
time: 587 us; the launch traced here: 581 us
  waiting for transfers between devices  462 us (79%)
  blocking collectives  40.5 us (7%)
  starting transfers between devices  27.9 us (5%)
  matrix products  16.9 us (3%)
  local copies, waits for them, and re-layouts  14.8 us (3%)
  between operations  14.3 us (2%)
    reduce_scatter x2, waiting for transfers between devices, sum_features(): lax.psum_scatter(terms(jnp.int32(0), rows * lax.axis_size('dp')), 'dp', s...  153 us
    reduce_scatter x2, waiting for transfers between devices, sum_units(): return lax.psum_scatter(values, 'et', scatter_dimension=1, tiled=True)  139 us
    all_gather x2, waiting for transfers between devices, gather_rows(): return lax.all_gather(values, 'dp', axis=0, tiled=True)  133 us
    all_to_all x2, waiting for transfers between devices, to_group_rows(): return lax.all_to_all(values, 'dp', split_axis=0, concat_axis=1, tiled=True)  37 us
    all_to_all x2, starting transfers between devices, to_group_rows(): return lax.all_to_all(values, 'dp', split_axis=0, concat_axis=1, tiled=True)  27.5 us
    all_to_all x1, blocking collectives, expert_pass(): lax.all_to_all(d_rows, 'dp', split_axis=1, concat_axis=0, tiled=True)  22 us
    all_to_all x1, blocking collectives, expert_pass(): lax.all_to_all(routed, 'dp', split_axis=1, concat_axis=0, tiled=True)  18.5 us
  transfers between devices with their start and end apart: 8, of which 8 were waited for; matrix products, arithmetic and copies ran while one was open for 5% of the time, Pallas kernels for 0%

commit v1 on v0

v1 whole, which is shorter than its diff:
```python
import jax
import jax.numpy as jnp
import numpy as np
from jax import lax
from jax.sharding import Mesh, PartitionSpec as P

CAP = 32
DP = ("zl", "y")
ET = ("zh", "x", "c")
ALL = DP + ET
SIZES = (4, 4, 2, 4, 2)
F32 = jnp.float32
BF16 = jnp.bfloat16


def route_table(expert_ids, gate_fixed, experts, capacity):
    expert_range = jnp.arange(experts, dtype=jnp.int32)
    picked = (expert_ids[None, :, :] == expert_range[:, None, None]).astype(jnp.int32)
    member = jnp.sum(picked, axis=2)
    scaled = jnp.sum(picked * gate_fixed[None, :, :], axis=2).astype(F32) / 32768.0
    before = jnp.cumsum(member, axis=1) - member
    slot_range = jnp.arange(capacity, dtype=jnp.int32)
    hit = (member[:, None, :] == 1) & (before[:, None, :] == slot_range[None, :, None])
    dispatch = hit.astype(F32)
    row_weight = jnp.sum(dispatch * scaled[:, None, :], axis=2)
    return dispatch, row_weight


def exchange(values, axes):
    return lax.all_to_all(values, axes, split_axis=0, concat_axis=0, tiled=True)


def dot(spec, left, right):
    return jnp.einsum(spec, left, right, preferred_element_type=F32)


def local(tokens, expert_ids, gate_fixed, w_gate, w_up, w_down, d_out):
    highest = lax.Precision.HIGHEST
    experts, width, units = w_gate.shape
    n_zl, n_y = lax.axis_size("zl"), lax.axis_size("y")
    n_dp = n_zl * n_y
    n_q = lax.axis_size("x") * lax.axis_size("c")
    n_et = n_q * lax.axis_size("zh")
    rows = experts * CAP
    share = rows // n_q
    quarter = n_q // experts
    sub = units // n_y
    token_rows = tokens.shape[0]

    dispatch, row_weight = route_table(expert_ids, gate_fixed, experts, CAP)
    flat_dispatch = dispatch.reshape(rows, token_rows)
    flat_weight = row_weight.reshape(rows)

    place = lax.axis_index(("x", "c"))
    my_dispatch = lax.dynamic_slice_in_dim(flat_dispatch, place * share, share, 0).astype(BF16)
    my_weight = lax.dynamic_slice_in_dim(flat_weight, place * share, share, 0)
    my_routed = jnp.dot(my_dispatch, tokens, preferred_element_type=F32).astype(BF16)
    my_grads = (my_weight[:, None] * jnp.dot(my_dispatch, d_out, preferred_element_type=F32)).astype(BF16)
    both = jnp.stack([my_routed, my_grads])
    both = both.reshape(2, share, n_zl, n_y * width).transpose(2, 0, 1, 3)
    both = jnp.broadcast_to(both[:, None], (n_zl, n_y, 2, share, n_y * width))
    both = exchange(both.reshape(n_dp, 2, share, n_y * width), DP)
    both = lax.all_gather(both, ("x", "c"), axis=0)
    both = both.reshape(experts, quarter, n_dp, 2, share, n_y * width)
    routed = both[:, :, :, 0].reshape(experts, quarter * n_dp * share, n_y, width)
    grads = both[:, :, :, 1].reshape(experts, quarter * n_dp * share, n_y, width)

    turned = jnp.stack([w_gate.transpose(0, 2, 1), w_up.transpose(0, 2, 1), w_down])
    turned = turned.reshape(3, experts, n_y, sub, width).transpose(2, 0, 1, 3, 4)
    turned = exchange(turned, "y")
    first = dot("smkfd,krsd->kmfr", turned[:, :2], routed)
    second = dot("skfd,krsd->kfr", turned[:, 2], grads)
    part = jnp.concatenate([first, second[:, None]], axis=1)
    part = part.reshape(experts, 3, sub, quarter, n_dp * share).transpose(3, 0, 1, 2, 4)
    summed = jnp.sum(exchange(part.astype(BF16), "zl").astype(F32), axis=0)
    gate, up, d_hidden = summed[:, 0], summed[:, 1], summed[:, 2]
    sigma = jax.nn.sigmoid(gate)
    hidden = (gate * sigma * up).astype(BF16)
    d_gate = (d_hidden * up * sigma * (1.0 + gate * (1.0 - sigma))).astype(BF16)
    d_up = (d_hidden * gate * sigma).astype(BF16)
    acts = jnp.stack([hidden, d_gate, d_up])
    acts = lax.all_gather(acts, DP, axis=0).reshape(n_zl, n_y, 3, experts, sub, n_dp * share)
    hidden, d_gate, d_up = acts[:, :, 0], acts[:, :, 1], acts[:, :, 2]

    y = lax.axis_index("y")
    routed = lax.dynamic_index_in_dim(routed, y, 2, keepdims=False)
    grads = lax.dynamic_index_in_dim(grads, y, 2, keepdims=False)
    routed = routed.reshape(experts, quarter, n_dp * share, width)
    grads = grads.reshape(experts, quarter, n_dp * share, width)
    blocks_down = w_down.reshape(experts, n_y, sub, width)
    blocks_gate = w_gate.reshape(experts, width, n_y, sub)
    blocks_up = w_up.reshape(experts, width, n_y, sub)
    down = dot("zykfr,kyfd->kzrd", hidden, blocks_down)
    back = dot("zykfr,kdyf->kzrd", d_gate, blocks_gate)
    back = back + dot("zykfr,kdyf->kzrd", d_up, blocks_up)
    grad_down = dot("zykfr,kzrd->kyfd", hidden, grads).reshape(experts, units, width)
    grad_gate = dot("kzrd,zykfr->kdyf", routed, d_gate).reshape(experts, width, units)
    grad_up = dot("kzrd,zykfr->kdyf", routed, d_up).reshape(experts, width, units)

    sums = jnp.stack([down, back]).reshape(2, experts, quarter, n_dp, share, width)
    sums = sums.transpose(3, 0, 1, 2, 4, 5).reshape(n_dp, 2, rows, width)
    sums = jnp.sum(exchange(sums, ET), axis=0)
    home = [(i * n_et + j, j * n_dp + i) for i in range(n_dp) for j in range(n_et)]
    sums = lax.ppermute(sums, ALL, home)
    weighted = flat_dispatch * flat_weight[:, None]
    mixed = jnp.einsum("rt,rd->td", weighted, sums[0], precision=highest)
    grad_tokens = jnp.einsum("rt,rd->td", flat_dispatch, sums[1], precision=highest)
    return mixed, grad_tokens, grad_gate, grad_up, grad_down


def solution(mesh):
    fine = Mesh(np.asarray(mesh.devices).reshape(SIZES), ALL)
    placed = (
        P(DP, None),
        P(DP, None),
        P(DP, None),
        P(None, DP, ET),
        P(None, DP, ET),
        P(None, ET, DP),
        P(DP, None),
    )
    return jax.shard_map(
        local,
        mesh=fine,
        in_specs=placed,
        out_specs=(P(DP, ET), P(DP, ET), P(None, DP, ET), P(None, DP, ET), P(None, ET, DP)),
        check_vma=False,
    )
```

time: 587 us -> 304 us (0.52)
  the two profiles are of different devices: /device:TPU:67 before, /device:TPU:94 now
where the time goes in v1:
time: 304 us
  waiting for transfers between devices  160 us (53%)
  blocking collectives  54.8 us (18%)
  local copies, waits for them, and re-layouts  35.3 us (12%)
  matrix products  18.9 us (6%)
  starting transfers between devices  17.5 us (6%)
  between operations  14.3 us (5%)
  other arithmetic  3.13 us (1%)
    all_gather x1, waiting for transfers between devices, local(): lax.all_gather(acts, DP, axis=0)  87.5 us
    all_to_all x2, blocking collectives, exchange(): return lax.all_to_all(values, axes, split_axis=0, concat_axis=0, tiled=True)  54.8 us
    all_to_all x2, waiting for transfers between devices, exchange(): return lax.all_to_all(values, axes, split_axis=0, concat_axis=0, tiled=True)  47.6 us
    all_gather x1, waiting for transfers between devices, local(): both = lax.all_gather(both, ('x', 'c'), axis=0)  21.9 us
    all_to_all x2, starting transfers between devices, exchange(): return lax.all_to_all(values, axes, split_axis=0, concat_axis=0, tiled=True)  15.6 us
    dot_general x8, matrix products, dot(): return jnp.einsum(spec, left, right, preferred_element_type=F32)  15.2 us
    unnamed x27, local copies, waits for them, and re-layouts  14 us
  transfers between devices with their start and end apart: 5, of which 4 were waited for; matrix products, arithmetic and copies ran while one was open for 11% of the time, Pallas kernels for 0%

profile of v1, /device:TPU:94, one launch (start us, length us, event | category | flops | bytes accessed | tf_op | source)
XLA Modules:
  0.0 303.8 jit_solution(2500840395585261375)
XLA Ops:
  7.2 0.0 copy-start
  7.2 0.0 all-gather.5.cloned.1.call-start
  7.2 0.8 convert_reduce_fusion.1
  8.0 0.3 reduce_window_sum.11
  8.3 0.1 eq.73
  8.4 0.1 select_reduce_fusion
  8.5 0.1 reshape.304
  8.6 0.1 dynamic-slice
  8.7 0.1 dynamic_slice.14
  8.8 0.3 convolution_convert_fusion
  9.1 1.5 fusion
  10.7 0.1 broadcast_in_dim.2
  10.7 19.2 %all_to_all.20 = bf16[16,2,8,1024]{3,2,1,0:T(8,128)(2,1)} all-to-all(bf16[16,2,8,1024]{3,2,1,0:T(8,128)(2,1)S(1)} %bitcast.186), channel_id=1, replica_groups=mesh['zl'=4,'y'=4,'zh'=2,'x'=4,'c'=2] {'zl','y'}, dimensions={0} | all-to-all | bytes 1048576 | tf_op jit(solution)/shard_map/all_to_all | solution.py:30
  29.9 0.0 all-gather.5.cloned.1.call-update
  29.9 0.0 copy-start.8
  29.9 1.5 copy.149
  31.5 0.0 copy-start.2
  31.5 1.8 copy.150
  33.3 0.3 maximum_bitcast_fusion
  33.6 1.8 copy.151
  35.4 8.2 %all-to-all-start = ((bf16[4,3,2,224,256]{4,3,1,2,0:T(8,128)(2,1)}), bf16[4,3,2,224,256]{4,3,1,2,0:T(8,128)(2,1)}, u32[]{:S(2)}, u32[]{:S(2)}) async-start(bf16[4,3,2,224,256]{4,3,1,2,0:T(8,128)(2,1)} %copy.151), calls=%async_computation | async-start | bytes 5505024 | tf_op jit(solution)/shard_map/all_to_all | solution.py:30
  43.6 0.0 all-gather.7.cloned.1.call-start
  43.6 21.9 %all-gather.5.cloned.1.call-done = bf16[128,2,8,1024]{3,2,1,0:T(8,128)(2,1)} async-done(((bf16[16,2,8,1024]{3,2,1,0:T(8,128)(2,1)}), bf16[128,2,8,1024]{3,2,1,0:T(8,128)(2,1)}) %all-gather.5.cloned.1.call-update) | async-done | bytes 4194320 | tf_op jit(solution)/shard_map/all_gather | solution.py:63
  65.5 4.3 %slice_bitcast_fusion.1 = (bf16[2,4,16,1,8,1024]{5,4,2,1,0,3:T(8,128)(2,1)}, bf16[2,4,16,1,8,1024]{5,4,2,1,0,3:T(8,128)(2,1)S(1)}) fusion(bf16[2,4,16,2,8,1024]{5,4,3,2,1,0:T(8,128)(2,1)} %bitcast.182), kind=kLoop, calls=%fused_computation.6 | loop fusion | bytes 8388608
  69.8 4.5 %reshape_squeeze.6 = bf16[2,512,4,256]{3,2,1,0:T(4,128)(2,1)} reshape(bf16[2,4,16,1,8,1024]{5,4,2,1,0,3:T(8,128)(2,1)} %get-tuple-element.48) | data formatting | bytes 4194304 | tf_op jit(solution)/shard_map/reshape;squeeze | solution.py:65
  74.3 2.7 reshape_squeeze.7
  77.1 0.0 all-to-all-done
  77.1 3.4 %fusion.24 = bf16[2,2,28,4,8,128]{5,4,3,2,1,0:T(8,128)(2,1)S(1)} fusion(bf16[2,512,4,256,1]{3,2,1,0,4:T(4,128)(2,1)} %bitcast.179, bf16[4,3,2,224,256]{4,3,1,2,0:T(8,128)(2,1)} %all-to-all-done), kind=kOutput, calls=%fused_computation.32 | convolution fusion | flops 939982848 | bytes 4849664 | tf_op jit(solution)/shard_map/smkfd,krsd->kmfr/dot_general | solution.py:34
  80.5 0.2 copy.252
  80.7 2.0 fusion.32
  82.7 0.1 concatenate.13
  82.8 0.1 copy.160
  82.9 0.1 maximum_bitcast_fusion.1
  83.0 35.6 %all_to_all.21 = bf16[4,2,3,224,128]{4,3,2,1,0:T(8,128)(2,1)S(1)} all-to-all(bf16[4,2,3,224,128]{4,3,2,1,0:T(8,128)(2,1)S(1)} %maximum_bitcast_fusion.1), channel_id=1, replica_groups=mesh['zl'=4,'y'=4,'zh'=2,'x'=4,'c'=2] {'zl'}, dimensions={0} | all-to-all | bytes 2752512 | tf_op jit(solution)/shard_map/all_to_all | solution.py:30
  118.6 0.2 convert_reduce_fusion
  118.9 0.1 multiply_convert_fusion.2
  119.0 0.8 pad_maximum_fusion.1
  119.8 0.0 all-gather.7.cloned.1.call-update
  119.8 87.5 %all-gather.7.cloned.1.call-done = bf16[48,2,224,128]{3,2,1,0:T(8,128)(2,1)} async-done(((bf16[3,2,224,128]{3,2,1,0:T(8,128)(2,1)}), bf16[48,2,224,128]{3,2,1,0:T(8,128)(2,1)}) %all-gather.7.cloned.1.call-update) | async-done | bytes 5505040 | tf_op jit(solution)/shard_map/all_gather | solution.py:82
  207.3 5.5 %slice_bitcast_fusion.11 = (bf16[4,4,2,224,128]{4,3,2,1,0:T(8,128)(2,1)}, bf16[4,4,2,224,128]{4,3,2,1,0:T(8,128)(2,1)}, bf16[4,4,2,224,128]{4,3,2,1,0:T(8,128)(2...) fusion(bf16[4,4,3,2,224,128]{5,4,3,2,1,0:T(8,128)(2,1)} %bitcas, ...), kind=kLoop, calls=%fused_computation.66 | loop fusion | bytes 16515072 | tf_op jit(solution)/shard_map/squeeze | solution.py:83
  212.9 0.9 fusion.20
  213.8 0.3 copy-done.9
  214.1 0.9 fusion.19
  215.0 0.9 fusion.23
  215.8 0.1 pad_maximum_fusion
  216.0 1.6 copy.192
  217.6 7.4 %all-to-all-start.3 = ((f32[16,2,64,256]{3,2,1,0:T(8,128)}), f32[16,2,64,256]{3,2,1,0:T(8,128)S(1)}, u32[]{:S(2)}, u32[]{:S(2)}) async-start(f32[16,2,64,256]{3,2,1,0:T(8,128)} %bitcast.171), calls=%async_computation.3 | async-start | bytes 4194304 | tf_op jit(solution)/shard_map/all_to_all | solution.py:30
  225.0 0.1 broadcast_select_fusion
  225.1 4.4 %constant_dynamic-slice_fusion = (bf16[2,512,1,256]{3,2,1,0:T(2,128)(2,1)S(1)}, bf16[2,512,1,256]{3,2,1,0:T(2,128)(2,1)S(1)}) fusion(bf16[2,512,4,256]{3,2,1,0:T(4,128)(2,1)} %reshape_squeeze.6, s32[]{:T(128)S(6)} %select_n.10, bf16[2,512,4,256]{3,2,1,0:T(4,128)(2,1)} %reshape_squeeze.7), kind=kLoop, calls=%fused_computation.61 | loop fusion | bytes 2097156 | tf_op jit(solution)/shard_map/jit(dynamic_index_in_dim)/dynamic_slice | solution.py:86
  229.4 0.0 copy-start.6
  229.4 0.1 copy.193
  229.5 0.1 copy.194
  229.6 1.3 copy-done.6
  230.9 1.9 fusion.9
  232.8 1.9 fusion.7
  234.7 47.6 %all-to-all-done.3 = f32[16,2,64,256]{3,2,1,0:T(8,128)S(1)} async-done(((f32[16,2,64,256]{3,2,1,0:T(8,128)}), f32[16,2,64,256]{3,2,1,0:T(8,128)S(1)}, u32[]{:S(2)}, u32[]{:S(2)}) %all-to-all-start.3) | async-done | bytes 2097184 | tf_op jit(solution)/shard_map/all_to_all | solution.py:30
  282.3 0.1 reduce_sum.49
  282.4 1.9 collective-permute-start
  284.4 3.4 %fusion.5 = f32[2,4,224,256,1]{3,2,4,1,0:T(8,128)} fusion(bf16[2,4,128,256,1]{3,2,1,4,0:T(8,128)(2,1)S(1)} %bitcast.187, bf16[4,4,2,224,128]{4,3,2,1,0:T(8,128)(2,1)} %get-tuple-element.42), kind=kOutput, calls=%fused_computation.12 | convolution fusion | flops 469762048 | bytes 4194304 | tf_op jit(solution)/shard_map/zykfr,kzrd->kyfd/dot_general | solution.py:34
  287.7 2.9 copy.175
  290.6 1.7 copy.174
  292.3 2.8 collective-permute-done
  295.0 1.0 fusion.36
  296.0 0.9 fusion.35
  (23 shorter events, 0.1 us)
Async XLA Ops:
  7.2 1.6 copy-start
  7.2 58.3 %all-gather.5.cloned.1.call-start = ((), (), s32[]{:S(2)}) async-start(), calls=%async_computation.4 | async-start | bytes 4718592 | tf_op jit(solution)/shard_map/all_gather | solution.py:63
  29.9 3.4 %copy-start.8 = (bf16[2,896,256]{2,1,0:T(8,128)(2,1)S(1)}, bf16[2,896,256]{2,1,0:T(8,128)(2,1)}, u32[]{:S(2)}) copy-start(bf16[2,896,256]{2,1,0:T(8,128)(2,1)} %param.12) | copy-start | bytes 2752516
  31.5 2.1 copy-start.2
  35.4 41.7 %all-to-all-start = ((bf16[4,3,2,224,256]{4,3,1,2,0:T(8,128)(2,1)}), bf16[4,3,2,224,256]{4,3,1,2,0:T(8,128)(2,1)}, u32[]{:S(2)}, u32[]{:S(2)}) async-start(bf16[4,3,2,224,256]{4,3,1,2,0:T(8,128)(2,1)} %copy.151), calls=%async_computation | async-start | bytes 5505024 | tf_op jit(solution)/shard_map/all_to_all | solution.py:30
  43.6 163.7 %all-gather.7.cloned.1.call-start = ((), (), s32[]{:S(2)}) async-start(), calls=%async_computation.5 | async-start | bytes 5849088 | tf_op jit(solution)/shard_map/all_gather | solution.py:82
  77.1 3.6 %copy-start.7 = (bf16[2,512,4,256]{3,2,1,0:T(4,128)(2,1)S(1)}, bf16[2,512,4,256]{3,2,1,0:T(4,128)(2,1)}, u32[]{:S(2)}) copy-start(bf16[2,512,4,256]{3,2,1,0:T(4,128)(2,1)} %reshape_squeeze.7) | copy-start | bytes 6291460
  207.3 5.6 %copy-start.3 = (bf16[2,256,896]{1,2,0:T(8,128)(2,1)S(1)}, bf16[2,256,896]{1,2,0:T(8,128)(2,1)}, u32[]{:S(2)}) copy-start(bf16[2,256,896]{1,2,0:T(8,128)(2,1)} %copy-done.2) | copy-start | bytes 2752516
  212.9 1.2 copy-start.9
  217.6 64.7 %all-to-all-start.3 = ((f32[16,2,64,256]{3,2,1,0:T(8,128)}), f32[16,2,64,256]{3,2,1,0:T(8,128)S(1)}, u32[]{:S(2)}, u32[]{:S(2)}) async-start(f32[16,2,64,256]{3,2,1,0:T(8,128)} %bitcast.171), calls=%async_computation.3 | async-start | bytes 4194304 | tf_op jit(solution)/shard_map/all_to_all | solution.py:30
  229.4 1.5 copy-start.6
  230.9 1.9 copy-start.5
  282.4 12.6 %collective-permute-start = (f32[2,64,256]{2,1,0:T(8,128)S(1)}, f32[2,64,256]{2,1,0:T(8,128)S(1)}, u32[]{:S(2)}, u32[]{:S(2)}) collective-permute-start(f32[2,64,256]{2,1,0:T(8,128)S(1)} %reduce_sum.49), channel_id=1, source_target_pairs={{0,0},{1,16},{2,32},{3,48},{4,64},{5,80},{6,96},{7,112},{8,128},{9... | collective-permute-start | bytes 393224 | tf_op jit(solution)/shard_map/ppermute | solution.py:104
  287.7 2.9 copy-start.4
  290.6 6.3 %copy-start.1 = (bf16[128,4096]{1,0:T(8,128)(2,1)S(1)}, bf16[128,4096]{1,0:T(8,128)(2,1)}, u32[]{:S(2)}) copy-start(bf16[128,4096]{1,0:T(8,128)(2,1)} %param.7) | copy-start | bytes 3145732
Sparse Core Ops, SparseCore 0:
  30.0 35.4 all-gather.4
  119.9 87.3 all-gather.6

commit v2 on v1

v2 whole, which is shorter than its diff:
```python
import jax
import jax.numpy as jnp
import numpy as np
from jax import lax
from jax.experimental import pallas as pl
from jax.experimental.pallas import tpu as pltpu
from jax.sharding import Mesh, PartitionSpec as P

CAP = 32
DP = ("zl", "y")
ET = ("zh", "x", "c")
ALL = DP + ET
SIZES = (4, 4, 2, 4, 2)
F32 = jnp.float32
BF16 = jnp.bfloat16
VMEM = pltpu.CompilerParams(vmem_limit_bytes=48 * 2**20)
NT = (((1,), (1,)), ((), ()))
TN = (((0,), (0,)), ((), ()))


def route_table(expert_ids, gate_fixed, experts, capacity):
    expert_range = jnp.arange(experts, dtype=jnp.int32)
    picked = (expert_ids[None, :, :] == expert_range[:, None, None]).astype(jnp.int32)
    member = jnp.sum(picked, axis=2)
    scaled = jnp.sum(picked * gate_fixed[None, :, :], axis=2).astype(F32) / 32768.0
    before = jnp.cumsum(member, axis=1) - member
    slot_range = jnp.arange(capacity, dtype=jnp.int32)
    hit = (member[:, None, :] == 1) & (before[:, None, :] == slot_range[None, :, None])
    dispatch = hit.astype(F32)
    row_weight = jnp.sum(dispatch * scaled[:, None, :], axis=2)
    return dispatch, row_weight


def exchange(values, axes):
    return lax.all_to_all(values, axes, split_axis=0, concat_axis=0, tiled=True)


def shift(values, axis, step):
    return lax.ppermute(values, axis, [(i, (i + step) % 4) for i in range(4)])


def spread(values, axis):
    return [values] + [shift(values, axis, step) for step in (1, 2, 3)]


def spread_ring(values, axis):
    half = values.shape[0] // 2
    left, right = shift(values, axis, 1), shift(values, axis, 3)
    far = (shift(left[:half], axis, 1), shift(right[half:], axis, 3))
    return (values, left, right) + far


def dot(left, right, dims):
    return lax.dot_general(left, right, dims, preferred_element_type=F32)


def call(body, out_shape, inputs, scratch=(), flops=0):
    outs = jax.tree.leaves(out_shape)
    size = sum(int(np.prod(a.shape)) * a.dtype.itemsize for a in list(inputs) + outs)
    return pl.pallas_call(
        body,
        in_specs=[pl.BlockSpec(memory_space=pltpu.SMEM)]
        + [pl.BlockSpec(memory_space=pltpu.VMEM)] * (len(inputs) - 1),
        out_specs=jax.tree.map(lambda _: pl.BlockSpec(memory_space=pltpu.VMEM), out_shape),
        out_shape=out_shape,
        scratch_shapes=list(scratch),
        compiler_params=VMEM,
        cost_estimate=pl.CostEstimate(flops=flops, bytes_accessed=size, transcendentals=0),
    )(*inputs)


def pick_kernel(q_ref, dispatch_ref, weight_ref, tokens_ref, cotangent_ref, *out_refs):
    routed = jnp.dot(dispatch_ref[...], tokens_ref[...], preferred_element_type=F32)
    grads = jnp.dot(dispatch_ref[...], cotangent_ref[...], preferred_element_type=F32)
    routed = routed.astype(BF16)
    grads = (weight_ref[...] * grads).astype(BF16)
    for k in range(2):
        for y in range(4):
            out_refs[k][0, y, 0] = routed[k * CAP : (k + 1) * CAP]
            out_refs[k][0, y, 1] = grads[k * CAP : (k + 1) * CAP]


def pick_rows(q, dispatch, weight, tokens, cotangent):
    rows, count = dispatch.shape
    return pl.pallas_call(
        pick_kernel,
        grid_spec=pltpu.PrefetchScalarGridSpec(
            num_scalar_prefetch=1,
            grid=(4,),
            in_specs=[
                pl.BlockSpec((rows, count), lambda z, q: (0, 0)),
                pl.BlockSpec((rows, 1), lambda z, q: (0, 0)),
                pl.BlockSpec((count, 128), lambda z, q: (0, z * 8 + q[0])),
                pl.BlockSpec((count, 128), lambda z, q: (0, z * 8 + q[0])),
            ],
            out_specs=[pl.BlockSpec((1, 4, 2, CAP, 128), lambda z, q: (z, 0, 0, 0, 0))] * 2,
        ),
        out_shape=[jax.ShapeDtypeStruct((4, 4, 2, CAP, 128), BF16)] * 2,
        compiler_params=VMEM,
    )(q, dispatch, weight, tokens, cotangent)


def slot_rows(x_ref, column, t):
    return x_ref[column, :, t].reshape(16 * CAP, 128)


def first_kernel(where_ref, x_ref, w_ref, part_ref, own_ref):
    zl = where_ref[0]
    sub = w_ref.shape[2]
    sums = [None, None]
    for s in range(4):
        for t in range(2):
            rows = jnp.concatenate([slot_rows(x_ref, 2 * s + h, t) for h in range(2)], axis=1)
            if t == 0:
                units = jnp.concatenate([w_ref[s, 0], w_ref[s, 1]], axis=0)
            else:
                units = w_ref[s, 2]
            term = dot(units, rows, NT)
            sums[t] = term if sums[t] is None else sums[t] + term
    for which in range(3):
        value = sums[which // 2]
        value = value[sub : 2 * sub] if which == 1 else value[:sub]
        for z in range(4):
            block = value[:, z * 128 : (z + 1) * 128]
            part_ref[(z - zl + 4) % 4, which] = block.astype(BF16)

            @pl.when(zl == z)
            def _():
                own_ref[which] = block


def first_products(where, x, w):
    sub = w.shape[2]
    out_shape = [
        jax.ShapeDtypeStruct((4, 3, sub, 128), BF16),
        jax.ShapeDtypeStruct((3, sub, 128), F32),
    ]
    return call(first_kernel, out_shape, (where, x, w), flops=2 * 512 * 1024 * 3 * sub)


def lanes(where_ref, refs, far, step, which):
    zl = where_ref[0]
    ref = (refs[0], refs[1], far, refs[2])[step]
    return jnp.concatenate([ref[(zl - z + 4) % 4, which] for z in range(4)], axis=1)


def join_far(refs, far):
    half = refs[3].shape[0]
    far[:half] = refs[3][...]
    far[half:] = refs[4][...]


def sums_kernel(where_ref, w_ref, r0, r1, r2, r3, r4, sums_ref, far):
    y = where_ref[1]
    refs = (r0, r1, r2, r3, r4)
    join_far(refs, far)
    down, back = None, None
    for step in (0, 1, 3, 2):
        at = (y - step + 4) % 4
        term = dot(lanes(where_ref, refs, far, step, 0), w_ref[at, 2], TN)
        down = term if down is None else down + term
        term = dot(lanes(where_ref, refs, far, step, 1), w_ref[at, 0], TN)
        term = term + dot(lanes(where_ref, refs, far, step, 2), w_ref[at, 1], TN)
        back = term if back is None else back + term
    for g in range(16):
        sums_ref[g % 8, g // 8, 0] = down[g * CAP : (g + 1) * CAP]
        sums_ref[g % 8, g // 8, 1] = back[g * CAP : (g + 1) * CAP]


def unit_sums(where, w, pieces):
    sub, width = w.shape[2:]
    out_shape = jax.ShapeDtypeStruct((8, 2, 2, CAP, width), F32)
    scratch = [pltpu.VMEM(pieces[0].shape, BF16)]
    return call(
        sums_kernel, out_shape, (where, w, *pieces), scratch, flops=2 * 512 * 12 * sub * width
    )


def grads_kernel(where_ref, *refs):
    x_refs, piece_refs, out_refs = refs[:2], (refs[2:7], refs[7:12]), refs[12:15]
    fars, units = refs[15:17], refs[17]
    gate_ref, up_ref, down_ref = out_refs
    y = where_ref[1]
    sub = units.shape[2]
    for k in range(2):
        join_far(piece_refs[k], fars[k])
        rows = [
            jnp.concatenate([slot_rows(x_refs[k], h, t) for h in range(2)], axis=1)
            for t in range(2)
        ]
        turned = rows[0].T
        for which, out_ref in ((0, down_ref), (1, gate_ref), (2, up_ref)):
            for step in range(4):
                at = (y - step + 4) % 4
                units[2 * which + k, at] = lanes(where_ref, piece_refs[k], fars[k], step, which)
            block = units[2 * which + k].reshape(4 * sub, 16 * CAP)
            if which == 0:
                out_ref[k] = jnp.dot(block, rows[1], preferred_element_type=F32)
            else:
                out_ref[k] = dot(turned, block, NT)


def weight_grads(where, columns, pieces):
    sub = pieces[0][0].shape[2]
    out_shape = [
        jax.ShapeDtypeStruct((2, 256, 4 * sub), F32),
        jax.ShapeDtypeStruct((2, 256, 4 * sub), F32),
        jax.ShapeDtypeStruct((2, 4 * sub, 256), F32),
    ]
    scratch = [pltpu.VMEM(pieces[0][0].shape, BF16)] * 2
    scratch.append(pltpu.VMEM((6, 4, sub, 16 * CAP), BF16))
    inputs = (where, *columns, *pieces[0], *pieces[1])
    return call(grads_kernel, out_shape, inputs, scratch, flops=2 * 1024 * 12 * sub * 256)


def local(tokens, expert_ids, gate_fixed, w_gate, w_up, w_down, d_out):
    highest = lax.Precision.HIGHEST
    experts, width, units = w_gate.shape
    n_y, n_dp, n_et = 4, 16, 16
    rows = experts * CAP
    sub = units // n_y
    zl, y, zh = lax.axis_index("zl"), lax.axis_index("y"), lax.axis_index("zh")
    where = jnp.stack([zl, y]).astype(jnp.int32)

    dispatch, row_weight = route_table(expert_ids, gate_fixed, experts, CAP)
    flat_dispatch = dispatch.reshape(rows, tokens.shape[0])
    flat_weight = row_weight.reshape(rows)

    q = lax.axis_index(("x", "c")).astype(jnp.int32).reshape(1)
    picked = pick_rows(q, flat_dispatch.astype(BF16), flat_weight[:, None], tokens, d_out)
    pairs = [(i, j) for i in range(n_dp) for j in range(n_et)]
    home_same = [(i * n_et + j, j * n_dp + i) for i, j in pairs]
    home_other = [(i * n_et + j, (j ^ 8) * n_dp + i) for i, j in pairs]

    columns, pieces, sums = [], [], []
    for k in range(experts):
        both = exchange(picked[k].reshape(n_dp, 2, CAP, 128), DP)
        both = lax.all_gather(both, ("x", "c"), axis=0)
        columns.append(lax.dynamic_slice_in_dim(both, 2 * y, 2, 0))

        held = jnp.stack([w_gate[k].T, w_up[k].T, w_down[k]])
        held = held.reshape(3, n_y, sub, width).transpose(1, 0, 2, 3)
        turned = exchange(held, "y")
        part, summed = first_products(where, both, turned)
        for step in (1, 2, 3):
            summed = summed + shift(part[step], "zl", step).astype(F32)
        gate, up, d_hidden = summed[0], summed[1], summed[2]
        sigma = jax.nn.sigmoid(gate)
        hidden = (gate * sigma * up).astype(BF16)
        d_gate = (d_hidden * up * sigma * (1.0 + gate * (1.0 - sigma))).astype(BF16)
        d_up = (d_hidden * gate * sigma).astype(BF16)
        acts = jnp.stack([hidden, d_gate, d_up])
        pieces.append(spread_ring(jnp.stack(spread(acts, "zl")), "y"))
        part = unit_sums(where, held, pieces[k])

        part = jnp.sum(exchange(part, ("x", "c")), axis=0)
        same = lax.dynamic_index_in_dim(part, zh, 0, keepdims=False)
        other = lax.dynamic_index_in_dim(part, 1 - zh, 0, keepdims=False)
        sums.append(lax.ppermute(same, ALL, home_same) + lax.ppermute(other, ALL, home_other))

    grad_gate, grad_up, grad_down = weight_grads(where, columns, pieces)
    sums = jnp.concatenate(sums, axis=1)
    weighted = flat_dispatch * flat_weight[:, None]
    mixed = jnp.einsum("rt,rd->td", weighted, sums[0], precision=highest)
    grad_tokens = jnp.einsum("rt,rd->td", flat_dispatch, sums[1], precision=highest)
    return mixed, grad_tokens, grad_gate, grad_up, grad_down


def solution(mesh):
    fine = Mesh(np.asarray(mesh.devices).reshape(SIZES), ALL)
    placed = (
        P(DP, None),
        P(DP, None),
        P(DP, None),
        P(None, DP, ET),
        P(None, DP, ET),
        P(None, ET, DP),
        P(DP, None),
    )
    return jax.shard_map(
        local,
        mesh=fine,
        in_specs=placed,
        out_specs=(P(DP, ET), P(DP, ET), P(None, DP, ET), P(None, DP, ET), P(None, ET, DP)),
        check_vma=False,
    )
```

time: 304 us -> 233 us (0.77)
  the two profiles are of different devices: /device:TPU:94 before, /device:TPU:67 now
where the time goes in v2:
time: 233 us; the launch traced here: 229 us
  waiting for transfers between devices  69.1 us (30%)
  starting transfers between devices  62.8 us (27%)
  blocking collectives  29.9 us (13%)
  local copies, waits for them, and re-layouts  27.3 us (12%)
  Pallas kernels  14.8 us (6%)
  between operations  14.5 us (6%)
  other arithmetic  9.16 us (4%)
    ppermute x20, waiting for transfers between devices, shift(): return lax.ppermute(values, axis, [(i, (i + step) % 4) for i in range(4)])  42.2 us
    all_to_all x2, blocking collectives, exchange(): return lax.all_to_all(values, axes, split_axis=0, concat_axis=0, tiled=True)  29.9 us
    all_to_all x4, waiting for transfers between devices, exchange(): return lax.all_to_all(values, axes, split_axis=0, concat_axis=0, tiled=True)  26.9 us
    all_to_all x4, starting transfers between devices, exchange(): return lax.all_to_all(values, axes, split_axis=0, concat_axis=0, tiled=True)  23.4 us
    ppermute x20, starting transfers between devices, shift(): return lax.ppermute(values, axis, [(i, (i + step) % 4) for i in range(4)])  21 us
    unnamed x36, local copies, waits for them, and re-layouts  17.6 us
    pallas_call x5, Pallas kernels, call(): pl.pallas_call(body, in_specs=[pl.BlockSpec(memory_space=pltpu.SMEM)] + [...  14.1 us
    ppermute x2, starting transfers between devices, local(): lax.ppermute(same, ALL, home_same) + lax.ppermute(other, ALL, home_other)  13.1 us
  transfers between devices with their start and end apart: 30, of which 12 were waited for; matrix products, arithmetic and copies ran while one was open for 8% of the time, Pallas kernels for 6%

profile of v2, /device:TPU:67, one launch (start us, length us, event | category | flops | bytes accessed | tf_op | source)
XLA Modules:
  0.0 229.5 jit_solution(16715051511766636696)
XLA Ops:
  8.7 1.2 copy-done.14
  9.9 1.2 copy-done.15
  11.9 16.6 %all_to_all.30 = bf16[16,2,32,128]{3,2,1,0:T(8,128)(2,1)} all-to-all(bf16[16,2,32,128]{3,2,1,0:T(8,128)(2,1)S(1)} %bitcast.86), channel_id=1, replica_groups=mesh['zl'=4,'y'=4,'zh'=2,'x'=4,'c'=2] {'zl','y'}, dimensions={0} | all-to-all | bytes 524288 | tf_op jit(solution)/shard_map/all_to_all | solution.py:35
  28.5 13.3 %all_to_all.31 = bf16[16,2,32,128]{3,2,1,0:T(8,128)(2,1)} all-to-all(bf16[16,2,32,128]{3,2,1,0:T(8,128)(2,1)S(1)} %bitcast.85), channel_id=1, replica_groups=mesh['zl'=4,'y'=4,'zh'=2,'x'=4,'c'=2] {'zl','y'}, dimensions={0} | all-to-all | bytes 524288 | tf_op jit(solution)/shard_map/all_to_all | solution.py:35
  42.1 0.9 copy-done.17
  43.3 1.2 fusion.14
  44.6 1.2 maximum_bitcast_fusion.w_ref
  45.8 3.5 %all-to-all-start.1 = ((bf16[4,3,224,256]{3,2,1,0:T(8,128)(2,1)}), bf16[4,3,224,256]{3,2,1,0:T(8,128)(2,1)S(1)}, u32[]{:S(2)}, u32[]{:S(2)}) async-start(bf16[4,3,224,256]{3,2,1,0:T(8,128)(2,1)} %maximum_bitcast_fusion.w_ref), calls=%async_computation.1 | async-start | bytes 2752512 | tf_op jit(solution)/shard_map/all_to_all | solution.py:35
  49.8 1.2 maximum_bitcast_fusion.1.w_ref
  51.0 15.6 %all-to-all-done.1.w_ref = bf16[4,3,224,256]{3,2,1,0:T(8,128)(2,1)S(1)} async-done(((bf16[4,3,224,256]{3,2,1,0:T(8,128)(2,1)}), bf16[4,3,224,256]{3,2,1,0:T(8,128)(2,1)S(1)}, u32[]{:S(2)}, u32[]{:S(2)}) %all-to-all-start.1) | async-done | bytes 1376288 | tf_op jit(solution)/shard_map/all_to_all | solution.py:35
  66.6 3.5 %all-to-all-start.4 = ((bf16[4,3,224,256]{3,2,1,0:T(8,128)(2,1)}), bf16[4,3,224,256]{3,2,1,0:T(8,128)(2,1)S(1)}, u32[]{:S(2)}, u32[]{:S(2)}) async-start(bf16[4,3,224,256]{3,2,1,0:T(8,128)(2,1)} %maximum_bitcast_fusion.1.w_ref), calls=%async_computation.4 | async-start | bytes 2752512 | tf_op jit(solution)/shard_map/all_to_all | solution.py:35
  70.2 1.7 copy-done.2
  71.9 1.7 shard_map.111
  75.2 11.3 %all-to-all-done.4.w_ref = bf16[4,3,224,256]{3,2,1,0:T(8,128)(2,1)S(1)} async-done(((bf16[4,3,224,256]{3,2,1,0:T(8,128)(2,1)}), bf16[4,3,224,256]{3,2,1,0:T(8,128)(2,1)S(1)}, u32[]{:S(2)}, u32[]{:S(2)}) %all-to-all-start.4) | async-done | bytes 1376288 | tf_op jit(solution)/shard_map/all_to_all | solution.py:35
  86.5 1.6 copy-done.3
  88.1 1.7 shard_map.113
  90.1 2.5 %collective-permute-start.4 = (bf16[3,224,128]{2,1,0:T(8,128)(2,1)S(1)}, bf16[3,224,128]{2,1,0:T(8,128)(2,1)S(1)}, u32[]{:S(2)}, u32[]{:S(2)}) collective-permute-start(bf16[3,224,128]{2,1,0:T(8,128)(2,1)S(1)} %get-tuple-element.46), channel_id=1, source_target_pairs={{0,128},{64,192},{128,0},{192,64},{1,129},{65,193},{129,1},{193,65... | collective-permute-start | bytes 516104 | tf_op jit(solution)/shard_map/ppermute | solution.py:39
  92.7 1.5 collective-permute-start.14
  94.2 1.8 collective-permute-start.13
  96.0 0.8 collective-permute-start.12
  96.8 3.4 %collective-permute-done.4 = bf16[3,224,128]{2,1,0:T(8,128)(2,1)S(1)} collective-permute-done((bf16[3,224,128]{2,1,0:T(8,128)(2,1)S(1)}, bf16[3,224,128]{2,1,0:T(8,128)(2,1)S(1)}, u32[]{:S(2)}, u32[]{:S(2)}) %collective-permute-start.4) | collective-permute-done | bytes 172064 | tf_op jit(solution)/shard_map/ppermute | solution.py:39
  100.2 15.7 %collective-permute-done.3 = bf16[3,224,128]{2,1,0:T(8,128)(2,1)S(1)} collective-permute-done((bf16[3,224,128]{2,1,0:T(8,128)(2,1)S(1)}, bf16[3,224,128]{2,1,0:T(8,128)(2,1)S(1)}, u32[]{:S(2)}, u32[]{:S(2)}) %collective-permute-start.3) | collective-permute-done | bytes 172064 | tf_op jit(solution)/shard_map/ppermute | solution.py:39
  116.0 0.8 collective-permute-start.6
  116.8 1.9 collective-permute-start.7
  118.8 4.5 %collective-permute-done.12 = bf16[3,224,128]{2,1,0:T(8,128)(2,1)S(1)} collective-permute-done((bf16[3,224,128]{2,1,0:T(8,128)(2,1)S(1)}, bf16[3,224,128]{2,1,0:T(8,128)(2,1)S(1)}, u32[]{:S(2)}, u32[]{:S(2)}) %collective-permute-start.12) | collective-permute-done | bytes 172064 | tf_op jit(solution)/shard_map/ppermute | solution.py:39
  123.7 1.4 collective-permute-start.15
  125.0 8.7 %collective-permute-done.6.r1.refs_3_ = bf16[4,3,224,128]{3,2,1,0:T(8,128)(2,1)S(1)} collective-permute-done((bf16[4,3,224,128]{3,2,1,0:T(8,128)(2,1)S(1)}, bf16[4,3,224,128]{3,2,1,0:T(8,128)(2,1)S(1)}, u32[]{:S(2)}, u32[]{:S(2)}) %collective-permute-start.6) | collective-permute-done | bytes 688160 | tf_op jit(solution)/shard_map/ppermute | solution.py:39
  133.8 2.7 %collective-permute-start.9 = (bf16[2,3,224,128]{3,2,1,0:T(8,128)(2,1)S(1)}, bf16[2,3,224,128]{3,2,1,0:T(8,128)(2,1)S(1)}, u32[]{:S(2)}, u32[]{:S(2)}) collective-permute-start(bf16[2,3,224,128]{3,2,1,0:T(8,128)(2,1)S(1)} %slice.100), channel_id=1, source_target_pairs={{0,48},{16,0},{32,16},{48,32},{1,49},{17,1},{33,17},{49,33},{2,50}... | collective-permute-start | bytes 1032200 | tf_op jit(solution)/shard_map/ppermute | solution.py:39
  136.6 1.6 collective-permute-done.16
  138.2 0.8 collective-permute-done.15
  139.1 1.0 collective-permute-start.18
  140.1 1.8 collective-permute-start.19
  141.9 1.2 collective-permute-done.8.r3.refs_5_
  143.1 2.5 %shard_map.112 = f32[8,2,2,32,256]{4,3,2,1,0:T(8,128)S(1)} custom-call(s32[2]{0:T(128)S(1)} %pad_add_fusion.where_ref, bf16[4,3,224,256]{3,2,1,0:T(8,128)(2,1)} %maximum_bitcast_fusion.w_ref, bf16[4,3,224,128]{3,2,1,0:T(8,128)(2,1)S(1)} %pad_maximum_fusion.r0.refs_2_, bf16[4,3,224,128]{3,2,1,0:T(8,128)(2,1)S(1)} %collective-permute-done.6.r1.refs_3_, ...), custom_call_target="tpu_custom_call" | custom-call | flops 704643072 | bytes 5177352 | tf_op jit(solution)/shard_map/pallas_call | solution.py:60
  145.6 1.0 copy-done.1
  147.3 0.8 copy-done.8
  148.1 8.4 %all-to-all-start.2 = ((f32[8,2,2,32,256]{4,3,2,1,0:T(8,128)}), f32[8,2,2,32,256]{4,3,2,1,0:T(8,128)}, u32[]{:S(2)}, u32[]{:S(2)}) async-start(f32[8,2,2,32,256]{4,3,2,1,0:T(8,128)} %copy-done.1), calls=%async_computation.2 | async-start | bytes 2097152 | tf_op jit(solution)/shard_map/all_to_all | solution.py:35
  156.5 1.5 collective-permute-done.18.r1.refs_8_
  158.1 1.0 slice.105
  159.1 2.7 %collective-permute-start.21 = (bf16[2,3,224,128]{3,2,1,0:T(8,128)(2,1)S(1)}, bf16[2,3,224,128]{3,2,1,0:T(8,128)(2,1)S(1)}, u32[]{:S(2)}, u32[]{:S(2)}) collective-permute-start(bf16[2,3,224,128]{3,2,1,0:T(8,128)(2,1)S(1)} %slice.105), channel_id=1, source_target_pairs={{0,48},{16,0},{32,16},{48,32},{1,49},{17,1},{33,17},{49,33},{2,50}... | collective-permute-start | bytes 1032200 | tf_op jit(solution)/shard_map/ppermute | solution.py:39
  161.8 4.7 %collective-permute-done.20.r3.refs_10_ = bf16[2,3,224,128]{3,2,1,0:T(8,128)(2,1)S(1)} collective-permute-done((bf16[2,3,224,128]{3,2,1,0:T(8,128)(2,1)S(1)}, bf16[2,3,224,128]{3,2,1,0:T(8,128)(2,1)S(1)}, u32[]{:S(2)}, u32[]{:S(2)}) %collective-permute-start.20) | collective-permute-done | bytes 344096 | tf_op jit(solution)/shard_map/ppermute | solution.py:39
  166.6 2.6 %shard_map.114 = f32[8,2,2,32,256]{4,3,2,1,0:T(8,128)S(1)} custom-call(s32[2]{0:T(128)S(1)} %pad_add_fusion.where_ref, bf16[4,3,224,256]{3,2,1,0:T(8,128)(2,1)} %maximum_bitcast_fusion.1.w_ref, bf16[4,3,224,128]{3,2,1,0:T(8,128)(2,1)S(1)} %pad_maximum_fusion.1.r0.refs_7_, bf16[4,3,224,128]{3,2,1,0:T(8,128)(2,1)S(1)} %collective-permute-done.18.r1.refs_8_, ...), custom_call_target="tpu_custom_call" | custom-call | flops 704643072 | bytes 5177352 | tf_op jit(solution)/shard_map/pallas_call | solution.py:60
  169.2 1.0 copy-done
  171.7 8.0 %all-to-all-start.5 = ((f32[8,2,2,32,256]{4,3,2,1,0:T(8,128)}), f32[8,2,2,32,256]{4,3,2,1,0:T(8,128)}, u32[]{:S(2)}, u32[]{:S(2)}) async-start(f32[8,2,2,32,256]{4,3,2,1,0:T(8,128)} %copy-done), calls=%async_computation.5 | async-start | bytes 2097152 | tf_op jit(solution)/shard_map/all_to_all | solution.py:35
  179.8 1.9 constant_dynamic-slice_fusion.1.refs_0_
  181.7 1.9 constant_dynamic-slice_fusion.refs_1_
  183.6 2.0 reduce_sum.48
  185.5 1.5 dynamic-slice_bitcast_fusion.2
  187.0 7.3 %collective-permute-start.10 = (f32[2,32,256]{2,1,0:T(8,128)}, f32[2,32,256]{2,1,0:T(8,128)S(1)}, u32[]{:S(2)}, u32[]{:S(2)}) collective-permute-start(f32[2,32,256]{2,1,0:T(8,128)} %get-tuple-element.50), channel_id=1, source_target_pairs={{0,0},{1,16},{2,32},{3,48},{4,64},{5,80},{6,96},{7,112},{8,128},{9... | collective-permute-start | bytes 196616 | tf_op jit(solution)/shard_map/ppermute | solution.py:259
  194.3 2.8 %collective-permute-start.11 = (f32[2,32,256]{2,1,0:T(8,128)}, f32[2,32,256]{2,1,0:T(8,128)}, u32[]{:S(2)}, u32[]{:S(2)}) collective-permute-start(f32[2,32,256]{2,1,0:T(8,128)} %get-tuple-element.49), channel_id=1, source_target_pairs={{0,128},{1,144},{2,160},{3,176},{4,192},{5,208},{6,224},{7,240},{8... | collective-permute-start | bytes 196616 | tf_op jit(solution)/shard_map/ppermute | solution.py:259
  197.1 2.0 reduce_sum.49
  199.1 0.9 dynamic-slice_bitcast_fusion
  200.0 5.8 %collective-permute-start.22 = (f32[2,32,256]{2,1,0:T(8,128)S(1)}, f32[2,32,256]{2,1,0:T(8,128)S(1)}, u32[]{:S(2)}, u32[]{:S(2)}) collective-permute-start(f32[2,32,256]{2,1,0:T(8,128)S(1)} %get-tuple-element.48), channel_id=1, source_target_pairs={{0,0},{1,16},{2,32},{3,48},{4,64},{5,80},{6,96},{7,112},{8,128},{9... | collective-permute-start | bytes 196616 | tf_op jit(solution)/shard_map/ppermute | solution.py:259
  205.8 2.4 %collective-permute-start.23 = (f32[2,32,256]{2,1,0:T(8,128)S(1)}, f32[2,32,256]{2,1,0:T(8,128)S(1)}, u32[]{:S(2)}, u32[]{:S(2)}) collective-permute-start(f32[2,32,256]{2,1,0:T(8,128)S(1)} %get-tuple-element.47), channel_id=1, source_target_pairs={{0,128},{1,144},{2,160},{3,176},{4,192},{5,208},{6,224},{7,240},{8... | collective-permute-start | bytes 196616 | tf_op jit(solution)/shard_map/ppermute | solution.py:259
  208.2 1.0 copy-done.4
  209.3 1.0 copy-done.5
  210.3 1.0 copy-done.7
  211.3 1.0 copy-done.9
  212.3 1.0 copy-done.11
  213.3 1.0 copy-done.13
  214.2 5.6 %shard_map.115 = (f32[2,256,896]{2,1,0:T(8,128)}, f32[2,256,896]{2,1,0:T(8,128)}, f32[2,896,256]{2,1,0:T(8,128)}) custom-call(s32[2]{0:T(128)S(1)} %pad_add_fusion.where_ref, bf16[2,16,2,32,128]{4,3,2,1,0:T(8,128)(2,1)S(1)} %copy-done.4, bf16[2,16,2,32,128]{4,3,2,1,0:T(8,128)(2,1)S(1)} %copy-done.5, bf16[4,3,224,128]{3,2,1,0:T(8,128)(2,1)S(1)} %pad_maximum_fusion.r0.refs_2_, ...), custom_call_target="tpu_custom_call" | custom-call | flops 1409286144 | bytes 12058632 | tf_op jit(solution)/shard_map/pallas_call | solution.py:60
  219.8 0.9 add.69
  220.7 1.0 fusion.2
  221.7 0.9 fusion.5
  (88 shorter events, 8.5 us)
Async XLA Ops:
  7.2 63.1 %all-gather.5.cloned.1.call-start = ((), (), s32[]{:S(2)}) async-start(), calls=%async_computation.6 | async-start | bytes 2359296 | tf_op jit(solution)/shard_map/all_gather | solution.py:238
  8.6 1.2 copy-start.14
  9.9 1.2 copy-start.15
  11.1 30.7 %copy-start.16 = (bf16[2,256,896]{2,1,0:T(8,128)(2,1)S(1)}, bf16[2,256,896]{2,1,0:T(8,128)(2,1)}, u32[]{:S(2)}) copy-start(bf16[2,256,896]{2,1,0:T(8,128)(2,1)} %param.11) | copy-start | bytes 2752516
  28.5 58.0 %all-gather.7.cloned.1.call-start = ((), (), s32[]{:S(2)}) async-start(), calls=%async_computation.7 | async-start | bytes 2359296 | tf_op jit(solution)/shard_map/all_gather | solution.py:238
  41.8 1.2 copy-start.17
  45.8 20.8 %all-to-all-start.1 = ((bf16[4,3,224,256]{3,2,1,0:T(8,128)(2,1)}), bf16[4,3,224,256]{3,2,1,0:T(8,128)(2,1)S(1)}, u32[]{:S(2)}, u32[]{:S(2)}) async-start(bf16[4,3,224,256]{3,2,1,0:T(8,128)(2,1)} %maximum_bitcast_fusion.w_ref), calls=%async_computation.1 | async-start | bytes 2752512 | tf_op jit(solution)/shard_map/all_to_all | solution.py:35
  66.6 19.9 %all-to-all-start.4 = ((bf16[4,3,224,256]{3,2,1,0:T(8,128)(2,1)}), bf16[4,3,224,256]{3,2,1,0:T(8,128)(2,1)S(1)}, u32[]{:S(2)}, u32[]{:S(2)}) async-start(bf16[4,3,224,256]{3,2,1,0:T(8,128)(2,1)} %maximum_bitcast_fusion.1.w_ref), calls=%async_computation.4 | async-start | bytes 2752512 | tf_op jit(solution)/shard_map/all_to_all | solution.py:35
  70.2 1.7 copy-start.2
  73.6 16.1 %collective-permute-start.2 = (bf16[3,224,128]{2,1,0:T(8,128)(2,1)S(1)}, bf16[3,224,128]{2,1,0:T(8,128)(2,1)S(1)}, u32[]{:S(2)}, u32[]{:S(2)}) collective-permute-start(bf16[3,224,128]{2,1,0:T(8,128)(2,1)S(1)} %get-tuple-element.35), channel_id=1, source_target_pairs={{0,192},{64,0},{128,64},{192,128},{1,193},{65,1},{129,65},{193,129... | collective-permute-start | bytes 516104 | tf_op jit(solution)/shard_map/ppermute | solution.py:39
  73.7 16.0 %collective-permute-start.1 = (bf16[3,224,128]{2,1,0:T(8,128)(2,1)S(1)}, bf16[3,224,128]{2,1,0:T(8,128)(2,1)S(1)}, u32[]{:S(2)}, u32[]{:S(2)}) collective-permute-start(bf16[3,224,128]{2,1,0:T(8,128)(2,1)S(1)} %get-tuple-element.36), channel_id=1, source_target_pairs={{0,128},{64,192},{128,0},{192,64},{1,129},{65,193},{129,1},{193,65... | collective-permute-start | bytes 516104 | tf_op jit(solution)/shard_map/ppermute | solution.py:39
  74.4 15.3 %collective-permute-start = (bf16[3,224,128]{2,1,0:T(8,128)(2,1)S(1)}, bf16[3,224,128]{2,1,0:T(8,128)(2,1)S(1)}, u32[]{:S(2)}, u32[]{:S(2)}) collective-permute-start(bf16[3,224,128]{2,1,0:T(8,128)(2,1)S(1)} %get-tuple-element.34), channel_id=1, source_target_pairs={{0,64},{64,128},{128,192},{192,0},{1,65},{65,129},{129,193},{193,1... | collective-permute-start | bytes 516104 | tf_op jit(solution)/shard_map/ppermute | solution.py:39
  86.5 1.6 copy-start.3
  90.0 6.0 %collective-permute-start.5 = (bf16[3,224,128]{2,1,0:T(8,128)(2,1)S(1)}, bf16[3,224,128]{2,1,0:T(8,128)(2,1)S(1)}, u32[]{:S(2)}, u32[]{:S(2)}) collective-permute-start(bf16[3,224,128]{2,1,0:T(8,128)(2,1)S(1)} %get-tuple-element.46), channel_id=1, source_target_pairs={{0,192},{64,0},{128,64},{192,128},{1,193},{65,1},{129,65},{193,129... | collective-permute-start | bytes 516104 | tf_op jit(solution)/shard_map/ppermute | solution.py:39
  90.1 10.2 %collective-permute-start.4 = (bf16[3,224,128]{2,1,0:T(8,128)(2,1)S(1)}, bf16[3,224,128]{2,1,0:T(8,128)(2,1)S(1)}, u32[]{:S(2)}, u32[]{:S(2)}) collective-permute-start(bf16[3,224,128]{2,1,0:T(8,128)(2,1)S(1)} %get-tuple-element.46), channel_id=1, source_target_pairs={{0,128},{64,192},{128,0},{192,64},{1,129},{65,193},{129,1},{193,65... | collective-permute-start | bytes 516104 | tf_op jit(solution)/shard_map/ppermute | solution.py:39
  92.6 23.3 %collective-permute-start.3 = (bf16[3,224,128]{2,1,0:T(8,128)(2,1)S(1)}, bf16[3,224,128]{2,1,0:T(8,128)(2,1)S(1)}, u32[]{:S(2)}, u32[]{:S(2)}) collective-permute-start(bf16[3,224,128]{2,1,0:T(8,128)(2,1)S(1)} %get-tuple-element.46), channel_id=1, source_target_pairs={{0,64},{64,128},{128,192},{192,0},{1,65},{65,129},{129,193},{193,1... | collective-permute-start | bytes 516104 | tf_op jit(solution)/shard_map/ppermute | solution.py:39
  92.7 26.1 %collective-permute-start.14 = (bf16[3,224,128]{2,1,0:T(8,128)(2,1)S(1)}, bf16[3,224,128]{2,1,0:T(8,128)(2,1)S(1)}, u32[]{:S(2)}, u32[]{:S(2)}) collective-permute-start(bf16[3,224,128]{2,1,0:T(8,128)(2,1)S(1)} %get-tuple-element.32), channel_id=1, source_target_pairs={{0,192},{64,0},{128,64},{192,128},{1,193},{65,1},{129,65},{193,129... | collective-permute-start | bytes 516104 | tf_op jit(solution)/shard_map/ppermute | solution.py:39
  94.2 24.6 %collective-permute-start.13 = (bf16[3,224,128]{2,1,0:T(8,128)(2,1)S(1)}, bf16[3,224,128]{2,1,0:T(8,128)(2,1)S(1)}, u32[]{:S(2)}, u32[]{:S(2)}) collective-permute-start(bf16[3,224,128]{2,1,0:T(8,128)(2,1)S(1)} %get-tuple-element.33), channel_id=1, source_target_pairs={{0,128},{64,192},{128,0},{192,64},{1,129},{65,193},{129,1},{193,65... | collective-permute-start | bytes 516104 | tf_op jit(solution)/shard_map/ppermute | solution.py:39
  96.0 27.3 %collective-permute-start.12 = (bf16[3,224,128]{2,1,0:T(8,128)(2,1)S(1)}, bf16[3,224,128]{2,1,0:T(8,128)(2,1)S(1)}, u32[]{:S(2)}, u32[]{:S(2)}) collective-permute-start(bf16[3,224,128]{2,1,0:T(8,128)(2,1)S(1)} %get-tuple-element.31), channel_id=1, source_target_pairs={{0,64},{64,128},{128,192},{192,0},{1,65},{65,129},{129,193},{193,1... | collective-permute-start | bytes 516104 | tf_op jit(solution)/shard_map/ppermute | solution.py:39
  116.0 17.7 %collective-permute-start.6 = (bf16[4,3,224,128]{3,2,1,0:T(8,128)(2,1)S(1)}, bf16[4,3,224,128]{3,2,1,0:T(8,128)(2,1)S(1)}, u32[]{:S(2)}, u32[]{:S(2)}) collective-permute-start(bf16[4,3,224,128]{3,2,1,0:T(8,128)(2,1)S(1)} %pad_maximum_fusion.r0.refs_2_), channel_id=1, source_target_pairs={{0,16},{16,32},{32,48},{48,0},{1,17},{17,33},{33,49},{49,1},{2,18}... | collective-permute-start | bytes 2064392 | tf_op jit(solution)/shard_map/ppermute | solution.py:39
  116.8 17.0 %collective-permute-start.7 = (bf16[4,3,224,128]{3,2,1,0:T(8,128)(2,1)S(1)}, bf16[4,3,224,128]{3,2,1,0:T(8,128)(2,1)S(1)}, u32[]{:S(2)}, u32[]{:S(2)}) collective-permute-start(bf16[4,3,224,128]{3,2,1,0:T(8,128)(2,1)S(1)} %pad_maximum_fusion.r0.refs_2_), channel_id=1, source_target_pairs={{0,48},{16,0},{32,16},{48,32},{1,49},{17,1},{33,17},{49,33},{2,50}... | collective-permute-start | bytes 2064392 | tf_op jit(solution)/shard_map/ppermute | solution.py:39
  123.5 13.1 %collective-permute-start.17 = (bf16[3,224,128]{2,1,0:T(8,128)(2,1)S(1)}, bf16[3,224,128]{2,1,0:T(8,128)(2,1)S(1)}, u32[]{:S(2)}, u32[]{:S(2)}) collective-permute-start(bf16[3,224,128]{2,1,0:T(8,128)(2,1)S(1)} %get-tuple-element.44), channel_id=1, source_target_pairs={{0,192},{64,0},{128,64},{192,128},{1,193},{65,1},{129,65},{193,129... | collective-permute-start | bytes 516104 | tf_op jit(solution)/shard_map/ppermute | solution.py:39
  123.6 14.6 %collective-permute-start.16 = (bf16[3,224,128]{2,1,0:T(8,128)(2,1)S(1)}, bf16[3,224,128]{2,1,0:T(8,128)(2,1)S(1)}, u32[]{:S(2)}, u32[]{:S(2)}) collective-permute-start(bf16[3,224,128]{2,1,0:T(8,128)(2,1)S(1)} %get-tuple-element.44), channel_id=1, source_target_pairs={{0,128},{64,192},{128,0},{192,64},{1,129},{65,193},{129,1},{193,65... | collective-permute-start | bytes 516104 | tf_op jit(solution)/shard_map/ppermute | solution.py:39
  123.7 15.4 %collective-permute-start.15 = (bf16[3,224,128]{2,1,0:T(8,128)(2,1)S(1)}, bf16[3,224,128]{2,1,0:T(8,128)(2,1)S(1)}, u32[]{:S(2)}, u32[]{:S(2)}) collective-permute-start(bf16[3,224,128]{2,1,0:T(8,128)(2,1)S(1)} %get-tuple-element.44), channel_id=1, source_target_pairs={{0,64},{64,128},{128,192},{192,0},{1,65},{65,129},{129,193},{193,1... | collective-permute-start | bytes 516104 | tf_op jit(solution)/shard_map/ppermute | solution.py:39
  133.7 9.4 %collective-permute-start.8 = (bf16[2,3,224,128]{3,2,1,0:T(8,128)(2,1)S(1)}, bf16[2,3,224,128]{3,2,1,0:T(8,128)(2,1)S(1)}, u32[]{:S(2)}, u32[]{:S(2)}) collective-permute-start(bf16[2,3,224,128]{3,2,1,0:T(8,128)(2,1)S(1)} %slice.99), channel_id=1, source_target_pairs={{0,16},{16,32},{32,48},{48,0},{1,17},{17,33},{33,49},{49,1},{2,18}... | collective-permute-start | bytes 1032200 | tf_op jit(solution)/shard_map/ppermute | solution.py:39
  133.8 9.3 %collective-permute-start.9 = (bf16[2,3,224,128]{3,2,1,0:T(8,128)(2,1)S(1)}, bf16[2,3,224,128]{3,2,1,0:T(8,128)(2,1)S(1)}, u32[]{:S(2)}, u32[]{:S(2)}) collective-permute-start(bf16[2,3,224,128]{3,2,1,0:T(8,128)(2,1)S(1)} %slice.100), channel_id=1, source_target_pairs={{0,48},{16,0},{32,16},{48,32},{1,49},{17,1},{33,17},{49,33},{2,50}... | collective-permute-start | bytes 1032200 | tf_op jit(solution)/shard_map/ppermute | solution.py:39
  139.1 18.8 %collective-permute-start.18 = (bf16[4,3,224,128]{3,2,1,0:T(8,128)(2,1)S(1)}, bf16[4,3,224,128]{3,2,1,0:T(8,128)(2,1)S(1)}, u32[]{:S(2)}, u32[]{:S(2)}) collective-permute-start(bf16[4,3,224,128]{3,2,1,0:T(8,128)(2,1)S(1)} %pad_maximum_fusion.1.r0.refs_7_), channel_id=1, source_target_pairs={{0,16},{16,32},{32,48},{48,0},{1,17},{17,33},{33,49},{49,1},{2,18}... | collective-permute-start | bytes 2064392 | tf_op jit(solution)/shard_map/ppermute | solution.py:39
  140.1 17.9 %collective-permute-start.19 = (bf16[4,3,224,128]{3,2,1,0:T(8,128)(2,1)S(1)}, bf16[4,3,224,128]{3,2,1,0:T(8,128)(2,1)}, u32[]{:S(2)}, u32[]{:S(2)}) collective-permute-start(bf16[4,3,224,128]{3,2,1,0:T(8,128)(2,1)S(1)} %pad_maximum_fusion.1.r0.refs_7_), channel_id=1, source_target_pairs={{0,48},{16,0},{32,16},{48,32},{1,49},{17,1},{33,17},{49,33},{2,50}... | collective-permute-start | bytes 2064392 | tf_op jit(solution)/shard_map/ppermute | solution.py:39
  145.6 1.0 copy-start.1
  146.6 0.7 copy-start.6
  147.3 0.8 copy-start.8
  148.1 23.7 %all-to-all-start.2 = ((f32[8,2,2,32,256]{4,3,2,1,0:T(8,128)}), f32[8,2,2,32,256]{4,3,2,1,0:T(8,128)}, u32[]{:S(2)}, u32[]{:S(2)}) async-start(f32[8,2,2,32,256]{4,3,2,1,0:T(8,128)} %copy-done.1), calls=%async_computation.2 | async-start | bytes 2097152 | tf_op jit(solution)/shard_map/all_to_all | solution.py:35
  158.0 8.6 %collective-permute-start.20 = (bf16[2,3,224,128]{3,2,1,0:T(8,128)(2,1)S(1)}, bf16[2,3,224,128]{3,2,1,0:T(8,128)(2,1)S(1)}, u32[]{:S(2)}, u32[]{:S(2)}) collective-permute-start(bf16[2,3,224,128]{3,2,1,0:T(8,128)(2,1)S(1)} %slice.104), channel_id=1, source_target_pairs={{0,16},{16,32},{32,48},{48,0},{1,17},{17,33},{33,49},{49,1},{2,18}... | collective-permute-start | bytes 1032200 | tf_op jit(solution)/shard_map/ppermute | solution.py:39
  159.1 7.5 %collective-permute-start.21 = (bf16[2,3,224,128]{3,2,1,0:T(8,128)(2,1)S(1)}, bf16[2,3,224,128]{3,2,1,0:T(8,128)(2,1)S(1)}, u32[]{:S(2)}, u32[]{:S(2)}) collective-permute-start(bf16[2,3,224,128]{3,2,1,0:T(8,128)(2,1)S(1)} %slice.105), channel_id=1, source_target_pairs={{0,48},{16,0},{32,16},{48,32},{1,49},{17,1},{33,17},{49,33},{2,50}... | collective-permute-start | bytes 1032200 | tf_op jit(solution)/shard_map/ppermute | solution.py:39
  169.2 1.0 copy-start
  170.2 0.8 copy-start.10
  171.0 0.8 copy-start.12
  171.7 25.4 %all-to-all-start.5 = ((f32[8,2,2,32,256]{4,3,2,1,0:T(8,128)}), f32[8,2,2,32,256]{4,3,2,1,0:T(8,128)}, u32[]{:S(2)}, u32[]{:S(2)}) async-start(f32[8,2,2,32,256]{4,3,2,1,0:T(8,128)} %copy-done), calls=%async_computation.5 | async-start | bytes 2097152 | tf_op jit(solution)/shard_map/all_to_all | solution.py:35
  187.0 32.8 %collective-permute-start.10 = (f32[2,32,256]{2,1,0:T(8,128)}, f32[2,32,256]{2,1,0:T(8,128)S(1)}, u32[]{:S(2)}, u32[]{:S(2)}) collective-permute-start(f32[2,32,256]{2,1,0:T(8,128)} %get-tuple-element.50), channel_id=1, source_target_pairs={{0,0},{1,16},{2,32},{3,48},{4,64},{5,80},{6,96},{7,112},{8,128},{9... | collective-permute-start | bytes 196616 | tf_op jit(solution)/shard_map/ppermute | solution.py:259
  194.3 25.5 %collective-permute-start.11 = (f32[2,32,256]{2,1,0:T(8,128)}, f32[2,32,256]{2,1,0:T(8,128)}, u32[]{:S(2)}, u32[]{:S(2)}) collective-permute-start(f32[2,32,256]{2,1,0:T(8,128)} %get-tuple-element.49), channel_id=1, source_target_pairs={{0,128},{1,144},{2,160},{3,176},{4,192},{5,208},{6,224},{7,240},{8... | collective-permute-start | bytes 196616 | tf_op jit(solution)/shard_map/ppermute | solution.py:259
  200.0 20.7 %collective-permute-start.22 = (f32[2,32,256]{2,1,0:T(8,128)S(1)}, f32[2,32,256]{2,1,0:T(8,128)S(1)}, u32[]{:S(2)}, u32[]{:S(2)}) collective-permute-start(f32[2,32,256]{2,1,0:T(8,128)S(1)} %get-tuple-element.48), channel_id=1, source_target_pairs={{0,0},{1,16},{2,32},{3,48},{4,64},{5,80},{6,96},{7,112},{8,128},{9... | collective-permute-start | bytes 196616 | tf_op jit(solution)/shard_map/ppermute | solution.py:259
  205.8 14.9 %collective-permute-start.23 = (f32[2,32,256]{2,1,0:T(8,128)S(1)}, f32[2,32,256]{2,1,0:T(8,128)S(1)}, u32[]{:S(2)}, u32[]{:S(2)}) collective-permute-start(f32[2,32,256]{2,1,0:T(8,128)S(1)} %get-tuple-element.47), channel_id=1, source_target_pairs={{0,128},{1,144},{2,160},{3,176},{4,192},{5,208},{6,224},{7,240},{8... | collective-permute-start | bytes 196616 | tf_op jit(solution)/shard_map/ppermute | solution.py:259
  208.2 1.0 copy-start.4
  209.3 1.0 copy-start.5
  210.3 1.0 copy-start.7
  211.3 1.0 copy-start.9
  212.3 1.0 copy-start.11
  213.3 1.0 copy-start.13
Sparse Core Ops, SparseCore 0:
  28.6 27.4 all-gather.4
  58.0 27.8 all-gather.6

commit v3 on v2

--- a/solution.py
+++ b/solution.py
@@ -43,11 +43,12 @@
     return [values] + [shift(values, axis, step) for step in (1, 2, 3)]
 
 
-def spread_ring(values, axis):
-    half = values.shape[0] // 2
-    left, right = shift(values, axis, 1), shift(values, axis, 3)
-    far = (shift(left[:half], axis, 1), shift(right[half:], axis, 3))
-    return (values, left, right) + far
+def after(values, *others):
+    return lax.optimization_barrier((values, *others))[0]
+
+
+def swap(values):
+    return lax.ppermute(values, "c", [(0, 1), (1, 0)])
 
 
 def dot(left, right, dims):
@@ -69,15 +70,14 @@
     )(*inputs)
 
 
-def pick_kernel(q_ref, dispatch_ref, weight_ref, tokens_ref, cotangent_ref, *out_refs):
+def pick_kernel(q_ref, dispatch_ref, weight_ref, tokens_ref, cotangent_ref, out_ref):
     routed = jnp.dot(dispatch_ref[...], tokens_ref[...], preferred_element_type=F32)
     grads = jnp.dot(dispatch_ref[...], cotangent_ref[...], preferred_element_type=F32)
     routed = routed.astype(BF16)
     grads = (weight_ref[...] * grads).astype(BF16)
-    for k in range(2):
-        for y in range(4):
-            out_refs[k][0, y, 0] = routed[k * CAP : (k + 1) * CAP]
-            out_refs[k][0, y, 1] = grads[k * CAP : (k + 1) * CAP]
+    for y in range(4):
+        out_ref[0, y, 0] = routed
+        out_ref[0, y, 1] = grads
 
 
 def pick_rows(q, dispatch, weight, tokens, cotangent):
@@ -93,49 +93,87 @@
                 pl.BlockSpec((count, 128), lambda z, q: (0, z * 8 + q[0])),
                 pl.BlockSpec((count, 128), lambda z, q: (0, z * 8 + q[0])),
             ],
-            out_specs=[pl.BlockSpec((1, 4, 2, CAP, 128), lambda z, q: (z, 0, 0, 0, 0))] * 2,
-        ),
-        out_shape=[jax.ShapeDtypeStruct((4, 4, 2, CAP, 128), BF16)] * 2,
+            out_specs=pl.BlockSpec((1, 4, 2, rows, 128), lambda z, q: (z, 0, 0, 0, 0)),
+        ),
+        out_shape=jax.ShapeDtypeStruct((4, 4, 2, rows, 128), BF16),
         compiler_params=VMEM,
     )(q, dispatch, weight, tokens, cotangent)
 
 
-def slot_rows(x_ref, column, t):
-    return x_ref[column, :, t].reshape(16 * CAP, 128)
-
-
-def first_kernel(where_ref, x_ref, w_ref, part_ref, own_ref):
-    zl = where_ref[0]
+def turn_kernel(where_ref, gate_ref, up_ref, down_ref, *held_refs):
+    for k, held_ref in enumerate(held_refs):
+        sub = held_ref.shape[2]
+        for which, ref in ((0, gate_ref), (1, up_ref)):
+            held_ref[:, which] = ref[k].T.reshape(4, sub, ref.shape[1])
+        held_ref[:, 2] = down_ref[k].reshape(4, sub, down_ref.shape[2])
+
+
+def turn_weights(where, w_gate, w_up, w_down):
+    experts, width, units = w_gate.shape
+    out_shape = [jax.ShapeDtypeStruct((4, 3, units // 4, width), BF16)] * experts
+    return call(turn_kernel, out_shape, (where, w_gate, w_up, w_down))
+
+
+def slot_rows(x_ref, t):
+    return jnp.concatenate([x_ref[h, :, t].reshape(16 * CAP, 128) for h in range(2)], axis=1)
+
+
+def first_kernel(where_ref, x_ref, w_ref, part_ref, own_ref, total):
+    zl, s = where_ref[0], pl.program_id(0)
     sub = w_ref.shape[2]
-    sums = [None, None]
-    for s in range(4):
-        for t in range(2):
-            rows = jnp.concatenate([slot_rows(x_ref, 2 * s + h, t) for h in range(2)], axis=1)
-            if t == 0:
-                units = jnp.concatenate([w_ref[s, 0], w_ref[s, 1]], axis=0)
-            else:
-                units = w_ref[s, 2]
-            term = dot(units, rows, NT)
-            sums[t] = term if sums[t] is None else sums[t] + term
-    for which in range(3):
-        value = sums[which // 2]
-        value = value[sub : 2 * sub] if which == 1 else value[:sub]
-        for z in range(4):
-            block = value[:, z * 128 : (z + 1) * 128]
-            part_ref[(z - zl + 4) % 4, which] = block.astype(BF16)
-
-            @pl.when(zl == z)
-            def _():
-                own_ref[which] = block
+    routed, grads = [slot_rows(x_ref, t) for t in range(2)]
+    first = dot(jnp.concatenate([w_ref[0, 0], w_ref[0, 1]], axis=0), routed, NT)
+    second = dot(w_ref[0, 2], grads, NT)
+
+    @pl.when(s == 0)
+    def _():
+        total[: 2 * sub] = first
+        total[2 * sub :] = second
+
+    @pl.when(s > 0)
+    def _():
+        total[: 2 * sub] += first
+        total[2 * sub :] += second
+
+    @pl.when(s == 3)
+    def _():
+        for which in range(3):
+            for z in range(4):
+                block = total[which * sub : (which + 1) * sub, z * 128 : (z + 1) * 128]
+                part_ref[(z - zl + 4) % 4, which] = block.astype(BF16)
+
+                @pl.when(zl == z)
+                def _():
+                    own_ref[which] = block
 
 
 def first_products(where, x, w):
-    sub = w.shape[2]
-    out_shape = [
-        jax.ShapeDtypeStruct((4, 3, sub, 128), BF16),
-        jax.ShapeDtypeStruct((3, sub, 128), F32),
-    ]
-    return call(first_kernel, out_shape, (where, x, w), flops=2 * 512 * 1024 * 3 * sub)
+    sub, width = w.shape[2:]
+    size = 2 * x.size + 2 * w.size + 10 * 3 * sub * 512
+    return pl.pallas_call(
+        first_kernel,
+        grid_spec=pltpu.PrefetchScalarGridSpec(
+            num_scalar_prefetch=1,
+            grid=(4,),
+            in_specs=[
+                pl.BlockSpec((2, 16, 2, CAP, 128), lambda s, where: (s, 0, 0, 0, 0)),
+                pl.BlockSpec((1, 3, sub, width), lambda s, where: (s, 0, 0, 0)),
+            ],
+            out_specs=[
+                pl.BlockSpec((4, 3, sub, 128), lambda s, where: (0, 0, 0, 0)),
+                pl.BlockSpec((3, sub, 128), lambda s, where: (0, 0, 0)),
+            ],
+            scratch_shapes=[pltpu.VMEM((3 * sub, 16 * CAP), F32)],
+        ),
+        out_shape=[
+            jax.ShapeDtypeStruct((4, 3, sub, 128), BF16),
+            jax.ShapeDtypeStruct((3, sub, 128), F32),
+        ],
+        compiler_params=VMEM,
+        cost_estimate=pl.CostEstimate(
+            flops=2 * 512 * 1024 * 3 * sub, bytes_accessed=size, transcendentals=0
+        ),
+    )(where, x, w)
 
 
 def lanes(where_ref, refs, far, step, which):
@@ -150,8 +188,8 @@
     far[half:] = refs[4][...]
 
 
-def sums_kernel(where_ref, w_ref, r0, r1, r2, r3, r4, sums_ref, far):
-    y = where_ref[1]
+def sums_kernel(where_ref, w_ref, r0, r1, r2, r3, r4, mine_ref, other_ref, far, held):
+    y, x, c, zh = where_ref[1], where_ref[2], where_ref[3], where_ref[4]
     refs = (r0, r1, r2, r3, r4)
     join_far(refs, far)
     down, back = None, None
@@ -163,14 +201,19 @@
         term = term + dot(lanes(where_ref, refs, far, step, 2), w_ref[at, 1], TN)
         back = term if back is None else back + term
     for g in range(16):
-        sums_ref[g % 8, g // 8, 0] = down[g * CAP : (g + 1) * CAP]
-        sums_ref[g % 8, g // 8, 1] = back[g * CAP : (g + 1) * CAP]
+        held[g, 0] = down[g * CAP : (g + 1) * CAP]
+        held[g, 1] = back[g * CAP : (g + 1) * CAP]
+    for step in range(4):
+        for turn in range(2):
+            g = ((zh + turn) % 2) * 8 + ((x + step) % 4) * 2
+            mine_ref[step, turn] = held[g + c]
+            other_ref[step, turn] = held[g + 1 - c]
 
 
 def unit_sums(where, w, pieces):
     sub, width = w.shape[2:]
-    out_shape = jax.ShapeDtypeStruct((8, 2, 2, CAP, width), F32)
-    scratch = [pltpu.VMEM(pieces[0].shape, BF16)]
+    out_shape = [jax.ShapeDtypeStruct((4, 2, 2, CAP, width), F32)] * 2
+    scratch = [pltpu.VMEM(pieces[0].shape, BF16), pltpu.VMEM((16, 2, CAP, width), F32)]
     return call(
         sums_kernel, out_shape, (where, w, *pieces), scratch, flops=2 * 512 * 12 * sub * width
     )
@@ -184,10 +227,7 @@
     sub = units.shape[2]
     for k in range(2):
         join_far(piece_refs[k], fars[k])
-        rows = [
-            jnp.concatenate([slot_rows(x_refs[k], h, t) for h in range(2)], axis=1)
-            for t in range(2)
-        ]
+        rows = [slot_rows(x_refs[k], t) for t in range(2)]
         turned = rows[0].T
         for which, out_ref in ((0, down_ref), (1, gate_ref), (2, up_ref)):
             for step in range(4):
@@ -200,7 +240,7 @@
                 out_ref[k] = dot(turned, block, NT)
 
 
-def weight_grads(where, columns, pieces):
+def weight_grads(where, x, pieces):
     sub = pieces[0][0].shape[2]
     out_shape = [
         jax.ShapeDtypeStruct((2, 256, 4 * sub), F32),
@@ -209,18 +249,31 @@
     ]
     scratch = [pltpu.VMEM(pieces[0][0].shape, BF16)] * 2
     scratch.append(pltpu.VMEM((6, 4, sub, 16 * CAP), BF16))
-    inputs = (where, *columns, *pieces[0], *pieces[1])
-    return call(grads_kernel, out_shape, inputs, scratch, flops=2 * 1024 * 12 * sub * 256)
+    whole = pl.BlockSpec(memory_space=pltpu.VMEM)
+    return pl.pallas_call(
+        grads_kernel,
+        grid_spec=pltpu.PrefetchScalarGridSpec(
+            num_scalar_prefetch=1,
+            grid=(1,),
+            in_specs=[pl.BlockSpec((2, 16, 2, CAP, 128), lambda i, where: (where[1], 0, 0, 0, 0))] * 2
+            + [whole] * 10,
+            out_specs=[whole] * 3,
+            scratch_shapes=scratch,
+        ),
+        out_shape=out_shape,
+        compiler_params=VMEM,
+        cost_estimate=pl.CostEstimate(
+            flops=2 * 1024 * 12 * sub * 256, bytes_accessed=12 * 2**20, transcendentals=0
+        ),
+    )(where, *x, *pieces[0], *pieces[1])
 
 
 def local(tokens, expert_ids, gate_fixed, w_gate, w_up, w_down, d_out):
     highest = lax.Precision.HIGHEST
     experts, width, units = w_gate.shape
-    n_y, n_dp, n_et = 4, 16, 16
+    n_dp, n_et = 16, 16
     rows = experts * CAP
-    sub = units // n_y
-    zl, y, zh = lax.axis_index("zl"), lax.axis_index("y"), lax.axis_index("zh")
-    where = jnp.stack([zl, y]).astype(jnp.int32)
+    where = jnp.stack([lax.axis_index(name) for name in ("zl", "y", "x", "c", "zh")]).astype(jnp.int32)
 
     dispatch, row_weight = route_table(expert_ids, gate_fixed, experts, CAP)
     flat_dispatch = dispatch.reshape(rows, tokens.shape[0])
@@ -232,34 +285,49 @@
     home_same = [(i * n_et + j, j * n_dp + i) for i, j in pairs]
     home_other = [(i * n_et + j, (j ^ 8) * n_dp + i) for i, j in pairs]
 
-    columns, pieces, sums = [], [], []
+    held = turn_weights(where, w_gate, w_up, w_down)
+    turned = [exchange(each, "y") for each in held]
+    sent = after(exchange(picked.reshape(n_dp, 2, rows, 128), DP), *held)
+    x = [lax.all_gather(sent[:, :, k * CAP : (k + 1) * CAP], ("x", "c"), axis=0) for k in range(experts)]
+    products = [first_products(where, x[k], turned[k]) for k in range(experts)]
+
+    pieces, sums = [], []
     for k in range(experts):
-        both = exchange(picked[k].reshape(n_dp, 2, CAP, 128), DP)
-        both = lax.all_gather(both, ("x", "c"), axis=0)
-        columns.append(lax.dynamic_slice_in_dim(both, 2 * y, 2, 0))
-
-        held = jnp.stack([w_gate[k].T, w_up[k].T, w_down[k]])
-        held = held.reshape(3, n_y, sub, width).transpose(1, 0, 2, 3)
-        turned = exchange(held, "y")
-        part, summed = first_products(where, both, turned)
+        part, summed = products[k]
         for step in (1, 2, 3):
             summed = summed + shift(part[step], "zl", step).astype(F32)
+        if k == 0:
+            summed = after(summed, turned[1])
         gate, up, d_hidden = summed[0], summed[1], summed[2]
         sigma = jax.nn.sigmoid(gate)
         hidden = (gate * sigma * up).astype(BF16)
         d_gate = (d_hidden * up * sigma * (1.0 + gate * (1.0 - sigma))).astype(BF16)
         d_up = (d_hidden * gate * sigma).astype(BF16)
         acts = jnp.stack([hidden, d_gate, d_up])
-        pieces.append(spread_ring(jnp.stack(spread(acts, "zl")), "y"))
-        part = unit_sums(where, held, pieces[k])
-
-        part = jnp.sum(exchange(part, ("x", "c")), axis=0)
-        same = lax.dynamic_index_in_dim(part, zh, 0, keepdims=False)
-        other = lax.dynamic_index_in_dim(part, 1 - zh, 0, keepdims=False)
-        sums.append(lax.ppermute(same, ALL, home_same) + lax.ppermute(other, ALL, home_other))
-
-    grad_gate, grad_up, grad_down = weight_grads(where, columns, pieces)
-    sums = jnp.concatenate(sums, axis=1)
+
+        lines = jnp.stack(spread(acts, "zl"))
+        if k == 0:
+            lines = after(lines, products[1][0])
+        left, right = shift(lines, "y", 1), shift(lines, "y", 3)
+        half = lines.shape[0] // 2
+        pieces.append([lines, left, right, shift(left[:half], "y", 1), shift(right[half:], "y", 3)])
+
+    grads = weight_grads(where, x, pieces)
+    for k in range(experts):
+        if k:
+            pieces[k][0] = after(pieces[k][0], part)
+        own, other = unit_sums(where, held[k], pieces[k])
+        own = own + swap(other)
+        part = own[0]
+        for step in (1, 2, 3):
+            part = part + shift(own[step], "x", step)
+        sums.append(part)
+    sums = jnp.concatenate(sums, axis=2).astype(BF16)
+    sums, *grads = lax.optimization_barrier((sums, *grads))
+    same, other = lax.ppermute(sums[0], ALL, home_same), lax.ppermute(sums[1], ALL, home_other)
+    sums = same.astype(F32) + other.astype(F32)
+
+    grad_gate, grad_up, grad_down = grads
     weighted = flat_dispatch * flat_weight[:, None]
     mixed = jnp.einsum("rt,rd->td", weighted, sums[0], precision=highest)
     grad_tokens = jnp.einsum("rt,rd->td", flat_dispatch, sums[1], precision=highest)

time: 233 us -> 219 us (0.940); the launches traced: 229 us -> 218 us
  waiting for transfers between devices: 69.1 us -> 92.9 us
  local copies, waits for them, and re-layouts: 27.3 us -> 10.5 us
  blocking collectives: 29.9 us -> 20.5 us
  starting transfers between devices: 62.8 us -> 55 us
  other arithmetic: 9.16 us -> 3.12 us
  Pallas kernels: 14.8 us -> 20.1 us
    ppermute x20 -> x26, waiting for transfers between devices: 42.2 us -> 63.4 us  [shift(): return lax.ppermute(values, axis, [(i, (i + step) % 4) for i in range(4)])]
    all_to_all x4 -> x2, waiting for transfers between devices: 26.9 us -> 11.2 us  [exchange(): return lax.all_to_all(values, axes, split_axis=0, concat_axis=0, tiled=True)]
    all_to_all x4 -> x2, starting transfers between devices: 23.4 us -> 11.2 us  [exchange(): return lax.all_to_all(values, axes, split_axis=0, concat_axis=0, tiled=True)]
    pallas_call x0 -> x3, Pallas kernels: none -> 11.8 us  [the longest x1 6.26 us: weight_grads(): pl.pallas_call(grads_kernel, grid_spec=pltpu.PrefetchScalarGridSpec(num_s...]
    ppermute x4, waiting for transfers between devices: 0.01 us -> 10.3 us  [the longest x1 8.79 us: local(): lax.ppermute(sums[0], ALL, home_same)]
    unnamed x36 -> x16, local copies, waits for them, and re-layouts: 17.6 us -> 8.15 us
    all_to_all x2 -> x1, blocking collectives: 29.9 us -> 20.5 us  [exchange(): return lax.all_to_all(values, axes, split_axis=0, concat_axis=0, tiled=True)]
    ppermute x20 -> x26, starting transfers between devices: 21 us -> 28.7 us  [shift(): return lax.ppermute(values, axis, [(i, (i + step) % 4) for i in range(4)])]
  transfers between devices with their start and end apart: 30 -> 34, of which waited for: 12 -> 18; matrix products, arithmetic and copies ran while one was open for 8% -> 0% of each run, Pallas kernels for 6% -> 7%
where the time goes in v3:
time: 219 us; the launch traced here: 218 us
  waiting for transfers between devices  92.9 us (42%)
  starting transfers between devices  55 us (25%)
  blocking collectives  20.5 us (9%)
  Pallas kernels  20.1 us (9%)
  between operations  14.4 us (7%)
  local copies, waits for them, and re-layouts  10.5 us (5%)
  other arithmetic  3.12 us (1%)
    ppermute x26, waiting for transfers between devices, shift(): return lax.ppermute(values, axis, [(i, (i + step) % 4) for i in range(4)])  63.4 us
    ppermute x26, starting transfers between devices, shift(): return lax.ppermute(values, axis, [(i, (i + step) % 4) for i in range(4)])  28.7 us
    all_to_all x1, blocking collectives, exchange(): return lax.all_to_all(values, axes, split_axis=0, concat_axis=0, tiled=True)  20.5 us
    all_to_all x2, waiting for transfers between devices, exchange(): return lax.all_to_all(values, axes, split_axis=0, concat_axis=0, tiled=True)  11.2 us
    all_to_all x2, starting transfers between devices, exchange(): return lax.all_to_all(values, axes, split_axis=0, concat_axis=0, tiled=True)  11.2 us
    ppermute x1, starting transfers between devices, local(): lax.ppermute(sums[1], ALL, home_other)  9.36 us
    ppermute x1, waiting for transfers between devices, local(): lax.ppermute(sums[0], ALL, home_same)  8.79 us
    unnamed x16, local copies, waits for them, and re-layouts  8.15 us
  transfers between devices with their start and end apart: 34, of which 18 were waited for; matrix products, arithmetic and copies ran while one was open for 0% of the time, Pallas kernels for 7%

profile of v3, /device:TPU:67, one launch (start us, length us, event | category | flops | bytes accessed | tf_op | source)
XLA Modules:
  0.0 218.4 jit_solution(14169567729379409703)
XLA Ops:
  7.2 0.7 convert_reduce_fusion
  7.9 0.3 reduce_window_sum.11
  8.6 1.2 copy-done.3
  9.8 1.2 copy-done.4
  11.1 1.9 shard_map.111
  12.9 7.6 %all-to-all-start = ((bf16[16,2,64,128]{3,2,1,0:T(8,128)(2,1)}), bf16[16,2,64,128]{3,2,1,0:T(8,128)(2,1)}, u32[]{:S(2)}, u32[]{:S(2)}) async-start(bf16[16,2,64,128]{3,2,1,0:T(8,128)(2,1)} %bitcast.9), calls=%async_computation | async-start | bytes 1048576 | tf_op jit(solution)/shard_map/all_to_all | solution.py:35
  20.7 1.2 copy-done.7
  21.9 2.2 shard_map.110
  24.0 11.2 %all-to-all-done = bf16[16,2,64,128]{3,2,1,0:T(8,128)(2,1)} async-done(((bf16[16,2,64,128]{3,2,1,0:T(8,128)(2,1)}), bf16[16,2,64,128]{3,2,1,0:T(8,128)(2,1)}, u32[]{:S(2)}, u32[]{:S(2)}) %all-to-all-start) | async-done | bytes 524320 | tf_op jit(solution)/shard_map/all_to_all | solution.py:35
  35.2 1.9 fusion.13
  37.2 0.7 all-gather.7.cloned.1.call-update
  37.9 20.5 %all_to_all.15.w_ref = bf16[4,3,224,256]{3,2,1,0:T(8,128)(2,1)} all-to-all(bf16[4,3,224,256]{3,2,1,0:T(8,128)(2,1)S(1)} %get-tuple-element.26.w_ref), channel_id=1, replica_groups=mesh['zl'=4,'y'=4,'zh'=2,'x'=4,'c'=2] {'y'}, dimensions={0} | all-to-all | bytes 2752512 | tf_op jit(solution)/shard_map/all_to_all | solution.py:35
  58.4 3.5 %all-to-all-start.2 = ((bf16[4,3,224,256]{3,2,1,0:T(8,128)(2,1)}), bf16[4,3,224,256]{3,2,1,0:T(8,128)(2,1)S(1)}, u32[]{:S(2)}, u32[]{:S(2)}) async-start(bf16[4,3,224,256]{3,2,1,0:T(8,128)(2,1)} %get-tuple-element.27.w_ref), calls=%async_computation.2 | async-start | bytes 2752512 | tf_op jit(solution)/shard_map/all_to_all | solution.py:35
  62.0 2.2 %all-gather.5.cloned.1.call-done = bf16[128,2,32,128]{3,2,1,0:T(8,128)(2,1)} async-done(((bf16[16,2,32,128]{3,2,1,0:T(8,128)(2,1)}), bf16[128,2,32,128]{3,2,1,0:T(8,128)(2,1)}) %all-gather.5.cloned.1.call-update) | async-done | bytes 2097168 | tf_op jit(solution)/shard_map/all_gather | solution.py:291
  64.2 1.6 copy-done
  65.8 1.3 copy-done.2
  67.1 2.8 %shard_map.112 = (bf16[4,3,224,128]{3,2,1,0:T(8,128)(2,1)S(1)}, f32[3,224,128]{2,1,0:T(8,128)S(1)}) custom-call(s32[5]{0:T(128)S(1)} %stack.65.where_ref, bf16[8,16,2,32,128]{4,3,2,1,0:T(8,128)(2,1)S(1)} %bitcast.84, bf16[4,3,224,256]{3,2,1,0:T(8,128)(2,1)S(1)} %copy-done.2), custom_call_target="tpu_custom_call" | custom-call | flops 704643072 | bytes 6914048 | tf_op jit(solution)/shard_map/pallas_call | solution.py:153
  69.9 0.3 collective-permute-start.2
  70.2 3.2 %collective-permute-start.1 = (bf16[3,224,128]{2,1,0:T(8,128)(2,1)S(1)}, bf16[3,224,128]{2,1,0:T(8,128)(2,1)S(1)}, u32[]{:S(2)}, u32[]{:S(2)}) collective-permute-start(bf16[3,224,128]{2,1,0:T(8,128)(2,1)S(1)} %get-tuple-element.51), channel_id=1, source_target_pairs={{0,128},{64,192},{128,0},{192,64},{1,129},{65,193},{129,1},{193,65... | collective-permute-start | bytes 516104 | tf_op jit(solution)/shard_map/ppermute | solution.py:39
  73.3 2.4 %collective-permute-done.2 = bf16[3,224,128]{2,1,0:T(8,128)(2,1)S(1)} collective-permute-done((bf16[3,224,128]{2,1,0:T(8,128)(2,1)S(1)}, bf16[3,224,128]{2,1,0:T(8,128)(2,1)S(1)}, u32[]{:S(2)}, u32[]{:S(2)}) %collective-permute-start.2) | collective-permute-done | bytes 172064 | tf_op jit(solution)/shard_map/ppermute | solution.py:39
  75.7 9.3 %collective-permute-done.1 = bf16[3,224,128]{2,1,0:T(8,128)(2,1)S(1)} collective-permute-done((bf16[3,224,128]{2,1,0:T(8,128)(2,1)S(1)}, bf16[3,224,128]{2,1,0:T(8,128)(2,1)S(1)}, u32[]{:S(2)}, u32[]{:S(2)}) %collective-permute-start.1) | collective-permute-done | bytes 172064 | tf_op jit(solution)/shard_map/ppermute | solution.py:39
  85.0 3.0 %collective-permute-done = bf16[3,224,128]{2,1,0:T(8,128)(2,1)S(1)} collective-permute-done((bf16[3,224,128]{2,1,0:T(8,128)(2,1)S(1)}, bf16[3,224,128]{2,1,0:T(8,128)(2,1)S(1)}, u32[]{:S(2)}, u32[]{:S(2)}) %collective-permute-start) | collective-permute-done | bytes 172064 | tf_op jit(solution)/shard_map/ppermute | solution.py:39
  88.5 1.4 collective-permute-start.3
  89.8 5.2 %all-gather.7.cloned.1.call-done = bf16[128,2,32,128]{3,2,1,0:T(8,128)(2,1)} async-done(((bf16[16,2,32,128]{3,2,1,0:T(8,128)(2,1)}), bf16[128,2,32,128]{3,2,1,0:T(8,128)(2,1)}) %all-gather.7.cloned.1.call-update) | async-done | bytes 2097168 | tf_op jit(solution)/shard_map/all_gather | solution.py:291
  95.0 1.6 copy-done.1
  96.6 2.8 %shard_map.113 = (bf16[4,3,224,128]{3,2,1,0:T(8,128)(2,1)S(1)}, f32[3,224,128]{2,1,0:T(8,128)S(1)}) custom-call(s32[5]{0:T(128)S(1)} %stack.65.where_ref, bf16[8,16,2,32,128]{4,3,2,1,0:T(8,128)(2,1)S(1)} %bitcast.86, bf16[4,3,224,256]{3,2,1,0:T(8,128)(2,1)S(1)} %all-to-all-done.2.w_ref), custom_call_target="tpu_custom_call" | custom-call | flops 704643072 | bytes 6914048 | tf_op jit(solution)/shard_map/pallas_call | solution.py:153
  99.4 2.8 %collective-permute-done.4 = bf16[3,224,128]{2,1,0:T(8,128)(2,1)} collective-permute-done((bf16[3,224,128]{2,1,0:T(8,128)(2,1)S(1)}, bf16[3,224,128]{2,1,0:T(8,128)(2,1)}, u32[]{:S(2)}, u32[]{:S(2)}) %collective-permute-start.4) | collective-permute-done | bytes 172064 | tf_op jit(solution)/shard_map/ppermute | solution.py:39
  102.2 2.2 %collective-permute-done.3 = bf16[3,224,128]{2,1,0:T(8,128)(2,1)} collective-permute-done((bf16[3,224,128]{2,1,0:T(8,128)(2,1)S(1)}, bf16[3,224,128]{2,1,0:T(8,128)(2,1)}, u32[]{:S(2)}, u32[]{:S(2)}) %collective-permute-start.3) | collective-permute-done | bytes 172064 | tf_op jit(solution)/shard_map/ppermute | solution.py:39
  104.4 1.1 pad_maximum_fusion.r0.refs_2_
  105.5 1.5 collective-permute-start.6
  107.0 1.2 collective-permute-start.7
  108.3 1.1 collective-permute-start.15
  109.5 1.4 collective-permute-start.14
  110.8 2.3 %collective-permute-done.16 = bf16[3,224,128]{2,1,0:T(8,128)(2,1)S(1)} collective-permute-done((bf16[3,224,128]{2,1,0:T(8,128)(2,1)S(1)}, bf16[3,224,128]{2,1,0:T(8,128)(2,1)S(1)}, u32[]{:S(2)}, u32[]{:S(2)}) %collective-permute-start.16) | collective-permute-done | bytes 172064 | tf_op jit(solution)/shard_map/ppermute | solution.py:39
  113.1 9.2 %collective-permute-done.15 = bf16[3,224,128]{2,1,0:T(8,128)(2,1)S(1)} collective-permute-done((bf16[3,224,128]{2,1,0:T(8,128)(2,1)S(1)}, bf16[3,224,128]{2,1,0:T(8,128)(2,1)S(1)}, u32[]{:S(2)}, u32[]{:S(2)}) %collective-permute-start.15) | collective-permute-done | bytes 172064 | tf_op jit(solution)/shard_map/ppermute | solution.py:39
  122.3 2.9 %collective-permute-done.14 = bf16[3,224,128]{2,1,0:T(8,128)(2,1)S(1)} collective-permute-done((bf16[3,224,128]{2,1,0:T(8,128)(2,1)S(1)}, bf16[3,224,128]{2,1,0:T(8,128)(2,1)S(1)}, u32[]{:S(2)}, u32[]{:S(2)}) %collective-permute-start.14) | collective-permute-done | bytes 172064 | tf_op jit(solution)/shard_map/ppermute | solution.py:39
  125.4 0.5 collective-permute-start.8
  125.9 2.5 %collective-permute-start.9 = (bf16[2,3,224,128]{3,2,1,0:T(8,128)(2,1)S(1)}, bf16[2,3,224,128]{3,2,1,0:T(8,128)(2,1)S(1)}, u32[]{:S(2)}, u32[]{:S(2)}) collective-permute-start(bf16[2,3,224,128]{3,2,1,0:T(8,128)(2,1)S(1)} %slice.121), channel_id=1, source_target_pairs={{0,48},{16,0},{32,16},{48,32},{1,49},{17,1},{33,17},{49,33},{2,50}... | collective-permute-start | bytes 1032200 | tf_op jit(solution)/shard_map/ppermute | solution.py:39
  128.6 0.3 collective-permute-start.18
  128.9 1.4 collective-permute-start.17
  130.3 5.7 %collective-permute-done.8.r3.refs_5_ = bf16[2,3,224,128]{3,2,1,0:T(8,128)(2,1)S(1)} collective-permute-done((bf16[2,3,224,128]{3,2,1,0:T(8,128)(2,1)S(1)}, bf16[2,3,224,128]{3,2,1,0:T(8,128)(2,1)S(1)}, u32[]{:S(2)}, u32[]{:S(2)}) %collective-permute-start.8) | collective-permute-done | bytes 344096 | tf_op jit(solution)/shard_map/ppermute | solution.py:39
  136.0 1.7 shard_map.114
  137.7 1.4 collective-permute-start.10
  139.2 3.4 %collective-permute-done.18 = bf16[3,224,128]{2,1,0:T(8,128)(2,1)S(1)} collective-permute-done((bf16[3,224,128]{2,1,0:T(8,128)(2,1)S(1)}, bf16[3,224,128]{2,1,0:T(8,128)(2,1)S(1)}, u32[]{:S(2)}, u32[]{:S(2)}) %collective-permute-start.18) | collective-permute-done | bytes 172064 | tf_op jit(solution)/shard_map/ppermute | solution.py:39
  142.6 2.5 %collective-permute-done.17 = bf16[3,224,128]{2,1,0:T(8,128)(2,1)S(1)} collective-permute-done((bf16[3,224,128]{2,1,0:T(8,128)(2,1)S(1)}, bf16[3,224,128]{2,1,0:T(8,128)(2,1)S(1)}, u32[]{:S(2)}, u32[]{:S(2)}) %collective-permute-start.17) | collective-permute-done | bytes 172064 | tf_op jit(solution)/shard_map/ppermute | solution.py:39
  145.3 2.7 %collective-permute-start.21 = (bf16[4,3,224,128]{3,2,1,0:T(8,128)(2,1)S(1)}, bf16[4,3,224,128]{3,2,1,0:T(8,128)(2,1)S(1)}, u32[]{:S(2)}, u32[]{:S(2)}) collective-permute-start(bf16[4,3,224,128]{3,2,1,0:T(8,128)(2,1)S(1)} %pad_maximum_fusion.1.r0.refs_7_), channel_id=1, source_target_pairs={{0,48},{16,0},{32,16},{48,32},{1,49},{17,1},{33,17},{49,33},{2,50}... | collective-permute-start | bytes 2064392 | tf_op jit(solution)/shard_map/ppermute | solution.py:39
  148.1 1.6 collective-permute-start.13
  149.7 1.1 collective-permute-start.12
  150.8 1.2 collective-permute-start.11
  152.0 11.0 %collective-permute-done.20.r1.refs_8_ = bf16[4,3,224,128]{3,2,1,0:T(8,128)(2,1)S(1)} collective-permute-done((bf16[4,3,224,128]{3,2,1,0:T(8,128)(2,1)S(1)}, bf16[4,3,224,128]{3,2,1,0:T(8,128)(2,1)S(1)}, u32[]{:S(2)}, u32[]{:S(2)}) %collective-permute-start.20) | collective-permute-done | bytes 688160 | tf_op jit(solution)/shard_map/ppermute | solution.py:39
  163.2 2.7 %collective-permute-start.23 = (bf16[2,3,224,128]{3,2,1,0:T(8,128)(2,1)S(1)}, bf16[2,3,224,128]{3,2,1,0:T(8,128)(2,1)S(1)}, u32[]{:S(2)}, u32[]{:S(2)}) collective-permute-start(bf16[2,3,224,128]{3,2,1,0:T(8,128)(2,1)S(1)} %slice.130), channel_id=1, source_target_pairs={{0,48},{16,0},{32,16},{48,32},{1,49},{17,1},{33,17},{49,33},{2,50}... | collective-permute-start | bytes 1032200 | tf_op jit(solution)/shard_map/ppermute | solution.py:39
  166.0 6.6 %collective-permute-done.22.r3.refs_10_ = bf16[2,3,224,128]{3,2,1,0:T(8,128)(2,1)S(1)} collective-permute-done((bf16[2,3,224,128]{3,2,1,0:T(8,128)(2,1)S(1)}, bf16[2,3,224,128]{3,2,1,0:T(8,128)(2,1)S(1)}, u32[]{:S(2)}, u32[]{:S(2)}) %collective-permute-start.22) | collective-permute-done | bytes 344096 | tf_op jit(solution)/shard_map/ppermute | solution.py:39
  172.6 2.5 %shard_map.115 = (f32[4,2,2,32,256]{4,3,2,1,0:T(8,128)S(1)}, f32[4,2,2,32,256]{4,3,2,1,0:T(8,128)S(1)}) custom-call(s32[5]{0:T(128)S(1)} %stack.65.where_ref, bf16[4,3,224,256]{3,2,1,0:T(8,128)(2,1)} %get-tuple-element.27.w_ref, bf16[4,3,224,128]{3,2,1,0:T(8,128)(2,1)S(1)} %pad_maximum_fusion.1.r0.refs_7_, ...), custom_call_target="tpu_custom_call" | custom-call | flops 704643072 | bytes 5177364 | tf_op jit(solution)/shard_map/pallas_call | solution.py:61
  175.1 2.3 %collective-permute-start.24 = (f32[4,2,2,32,256]{4,3,2,1,0:T(8,128)S(1)}, f32[4,2,2,32,256]{4,3,2,1,0:T(8,128)S(1)}, u32[]{:S(2)}, u32[]{:S(2)}) collective-permute-start(f32[4,2,2,32,256]{4,3,2,1,0:T(8,128)S(1)} %get-tuple-element.39), channel_id=1, source_target_pairs={{0,1},{1,0},{2,3},{3,2},{4,5},{5,4},{6,7},{7,6},{8,9},{9,8},{10,11... | collective-permute-start | bytes 1572872 | tf_op jit(solution)/shard_map/ppermute | solution.py:51
  177.5 1.5 collective-permute-done.24
  179.1 1.8 collective-permute-start.27
  181.0 1.1 collective-permute-start.26
  182.1 1.2 collective-permute-start.25
  183.2 6.3 %shard_map.116 = (f32[2,256,896]{2,1,0:T(8,128)}, f32[2,256,896]{2,1,0:T(8,128)}, f32[2,896,256]{2,1,0:T(8,128)}) custom-call(s32[5]{0:T(128)S(1)} %stack.65.where_ref, bf16[8,16,2,32,128]{4,3,2,1,0:T(8,128)(2,1)} %bitcast.83, bf16[8,16,2,32,128]{4,3,2,1,0:T(8,128)(2,1)} %bitcast.85, bf16[4,3,224,128]{3,2,1,0:T(8,128)(2,1)S(1)} %pad_maximum_fusion.r0.refs_2_, ...), custom_call_target="tpu_custom_call" | custom-call | flops 1409286144 | bytes 12582912 | tf_op jit(solution)/shard_map/pallas_call | solution.py:253
  189.6 9.4 %collective-permute-start.29 = (bf16[2,64,256]{2,1,0:T(8,128)(2,1)S(1)}, bf16[2,64,256]{2,1,0:T(8,128)(2,1)S(1)}, u32[]{:S(2)}, u32[]{:S(2)}) collective-permute-start(bf16[2,64,256]{2,1,0:T(8,128)(2,1)S(1)} %get-tuple-element.74), channel_id=1, source_target_pairs={{0,128},{1,144},{2,160},{3,176},{4,192},{5,208},{6,224},{7,240},{8... | collective-permute-start | bytes 196616 | tf_op jit(solution)/shard_map/ppermute | solution.py:327
  199.0 1.9 collective-permute-start.28
  200.9 8.8 %collective-permute-done.28 = bf16[2,64,256]{2,1,0:T(8,128)(2,1)S(1)} collective-permute-done((bf16[2,64,256]{2,1,0:T(8,128)(2,1)S(1)}, bf16[2,64,256]{2,1,0:T(8,128)(2,1)S(1)}, u32[]{:S(2)}, u32[]{:S(2)}) %collective-permute-start.28) | collective-permute-done | bytes 65568 | tf_op jit(solution)/shard_map/ppermute | solution.py:327
  209.7 1.0 fusion.8
  210.7 0.9 fusion.7
  (69 shorter events, 2.3 us)
Async XLA Ops:
  8.6 1.2 copy-start.3
  9.8 1.2 copy-start.4
  11.1 9.6 %copy-start.5 = (bf16[2,256,896]{2,1,0:T(8,128)(2,1)S(1)}, bf16[2,256,896]{2,1,0:T(8,128)(2,1)}, u32[]{:S(2)}) copy-start(bf16[2,256,896]{2,1,0:T(8,128)(2,1)} %gate_ref.1) | copy-start | bytes 2752516
  11.1 9.6 %copy-start.6 = (bf16[2,256,896]{2,1,0:T(8,128)(2,1)S(1)}, bf16[2,256,896]{2,1,0:T(8,128)(2,1)}, u32[]{:S(2)}) copy-start(bf16[2,256,896]{2,1,0:T(8,128)(2,1)} %up_ref.1) | copy-start | bytes 2752516
  12.9 22.3 %all-to-all-start = ((bf16[16,2,64,128]{3,2,1,0:T(8,128)(2,1)}), bf16[16,2,64,128]{3,2,1,0:T(8,128)(2,1)}, u32[]{:S(2)}, u32[]{:S(2)}) async-start(bf16[16,2,64,128]{3,2,1,0:T(8,128)(2,1)} %bitcast.9), calls=%async_computation | async-start | bytes 1048576 | tf_op jit(solution)/shard_map/all_to_all | solution.py:35
  20.6 43.6 %all-gather.5.cloned.1.call-start = ((), (), s32[]{:S(2)}) async-start(), calls=%async_computation.3 | async-start | bytes 2359296 | tf_op jit(solution)/shard_map/all_gather | solution.py:291
  20.7 1.2 copy-start.7
  37.1 57.9 %all-gather.7.cloned.1.call-start = ((), (), s32[]{:S(2)}) async-start(), calls=%async_computation.4 | async-start | bytes 2359296 | tf_op jit(solution)/shard_map/all_gather | solution.py:291
  58.4 29.6 %all-to-all-start.2 = ((bf16[4,3,224,256]{3,2,1,0:T(8,128)(2,1)}), bf16[4,3,224,256]{3,2,1,0:T(8,128)(2,1)S(1)}, u32[]{:S(2)}, u32[]{:S(2)}) async-start(bf16[4,3,224,256]{3,2,1,0:T(8,128)(2,1)} %get-tuple-element.27.w_ref), calls=%async_computation.2 | async-start | bytes 2752512 | tf_op jit(solution)/shard_map/all_to_all | solution.py:35
  64.2 1.6 copy-start
  65.8 1.3 copy-start.2
  69.9 5.8 %collective-permute-start.2 = (bf16[3,224,128]{2,1,0:T(8,128)(2,1)S(1)}, bf16[3,224,128]{2,1,0:T(8,128)(2,1)S(1)}, u32[]{:S(2)}, u32[]{:S(2)}) collective-permute-start(bf16[3,224,128]{2,1,0:T(8,128)(2,1)S(1)} %get-tuple-element.50), channel_id=1, source_target_pairs={{0,192},{64,0},{128,64},{192,128},{1,193},{65,1},{129,65},{193,129... | collective-permute-start | bytes 516104 | tf_op jit(solution)/shard_map/ppermute | solution.py:39
  70.2 14.8 %collective-permute-start.1 = (bf16[3,224,128]{2,1,0:T(8,128)(2,1)S(1)}, bf16[3,224,128]{2,1,0:T(8,128)(2,1)S(1)}, u32[]{:S(2)}, u32[]{:S(2)}) collective-permute-start(bf16[3,224,128]{2,1,0:T(8,128)(2,1)S(1)} %get-tuple-element.51), channel_id=1, source_target_pairs={{0,128},{64,192},{128,0},{192,64},{1,129},{65,193},{129,1},{193,65... | collective-permute-start | bytes 516104 | tf_op jit(solution)/shard_map/ppermute | solution.py:39
  73.3 14.6 %collective-permute-start = (bf16[3,224,128]{2,1,0:T(8,128)(2,1)S(1)}, bf16[3,224,128]{2,1,0:T(8,128)(2,1)S(1)}, u32[]{:S(2)}, u32[]{:S(2)}) collective-permute-start(bf16[3,224,128]{2,1,0:T(8,128)(2,1)S(1)} %get-tuple-element.49), channel_id=1, source_target_pairs={{0,64},{64,128},{128,192},{192,0},{1,65},{65,129},{129,193},{193,1... | collective-permute-start | bytes 516104 | tf_op jit(solution)/shard_map/ppermute | solution.py:39
  88.2 11.2 %collective-permute-start.5 = (bf16[3,224,128]{2,1,0:T(8,128)(2,1)S(1)}, bf16[3,224,128]{2,1,0:T(8,128)(2,1)S(1)}, u32[]{:S(2)}, u32[]{:S(2)}) collective-permute-start(bf16[3,224,128]{2,1,0:T(8,128)(2,1)S(1)} %get-tuple-element.70), channel_id=1, source_target_pairs={{0,192},{64,0},{128,64},{192,128},{1,193},{65,1},{129,65},{193,129... | collective-permute-start | bytes 516104 | tf_op jit(solution)/shard_map/ppermute | solution.py:39
  88.3 13.9 %collective-permute-start.4 = (bf16[3,224,128]{2,1,0:T(8,128)(2,1)S(1)}, bf16[3,224,128]{2,1,0:T(8,128)(2,1)}, u32[]{:S(2)}, u32[]{:S(2)}) collective-permute-start(bf16[3,224,128]{2,1,0:T(8,128)(2,1)S(1)} %get-tuple-element.70), channel_id=1, source_target_pairs={{0,128},{64,192},{128,0},{192,64},{1,129},{65,193},{129,1},{193,65... | collective-permute-start | bytes 516104 | tf_op jit(solution)/shard_map/ppermute | solution.py:39
  88.5 15.9 %collective-permute-start.3 = (bf16[3,224,128]{2,1,0:T(8,128)(2,1)S(1)}, bf16[3,224,128]{2,1,0:T(8,128)(2,1)}, u32[]{:S(2)}, u32[]{:S(2)}) collective-permute-start(bf16[3,224,128]{2,1,0:T(8,128)(2,1)S(1)} %get-tuple-element.70), channel_id=1, source_target_pairs={{0,64},{64,128},{128,192},{192,0},{1,65},{65,129},{129,193},{193,1... | collective-permute-start | bytes 516104 | tf_op jit(solution)/shard_map/ppermute | solution.py:39
  95.0 1.6 copy-start.1
  105.5 19.9 %collective-permute-start.6 = (bf16[4,3,224,128]{3,2,1,0:T(8,128)(2,1)S(1)}, bf16[4,3,224,128]{3,2,1,0:T(8,128)(2,1)S(1)}, u32[]{:S(2)}, u32[]{:S(2)}) collective-permute-start(bf16[4,3,224,128]{3,2,1,0:T(8,128)(2,1)S(1)} %pad_maximum_fusion.r0.refs_2_), channel_id=1, source_target_pairs={{0,16},{16,32},{32,48},{48,0},{1,17},{17,33},{33,49},{49,1},{2,18}... | collective-permute-start | bytes 2064392 | tf_op jit(solution)/shard_map/ppermute | solution.py:39
  107.0 18.9 %collective-permute-start.7 = (bf16[4,3,224,128]{3,2,1,0:T(8,128)(2,1)S(1)}, bf16[4,3,224,128]{3,2,1,0:T(8,128)(2,1)S(1)}, u32[]{:S(2)}, u32[]{:S(2)}) collective-permute-start(bf16[4,3,224,128]{3,2,1,0:T(8,128)(2,1)S(1)} %pad_maximum_fusion.r0.refs_2_), channel_id=1, source_target_pairs={{0,48},{16,0},{32,16},{48,32},{1,49},{17,1},{33,17},{49,33},{2,50}... | collective-permute-start | bytes 2064392 | tf_op jit(solution)/shard_map/ppermute | solution.py:39
  108.2 4.9 %collective-permute-start.16 = (bf16[3,224,128]{2,1,0:T(8,128)(2,1)S(1)}, bf16[3,224,128]{2,1,0:T(8,128)(2,1)S(1)}, u32[]{:S(2)}, u32[]{:S(2)}) collective-permute-start(bf16[3,224,128]{2,1,0:T(8,128)(2,1)S(1)} %get-tuple-element.53), channel_id=1, source_target_pairs={{0,192},{64,0},{128,64},{192,128},{1,193},{65,1},{129,65},{193,129... | collective-permute-start | bytes 516104 | tf_op jit(solution)/shard_map/ppermute | solution.py:39
  108.3 14.0 %collective-permute-start.15 = (bf16[3,224,128]{2,1,0:T(8,128)(2,1)S(1)}, bf16[3,224,128]{2,1,0:T(8,128)(2,1)S(1)}, u32[]{:S(2)}, u32[]{:S(2)}) collective-permute-start(bf16[3,224,128]{2,1,0:T(8,128)(2,1)S(1)} %get-tuple-element.54), channel_id=1, source_target_pairs={{0,128},{64,192},{128,0},{192,64},{1,129},{65,193},{129,1},{193,65... | collective-permute-start | bytes 516104 | tf_op jit(solution)/shard_map/ppermute | solution.py:39
  109.5 15.8 %collective-permute-start.14 = (bf16[3,224,128]{2,1,0:T(8,128)(2,1)S(1)}, bf16[3,224,128]{2,1,0:T(8,128)(2,1)S(1)}, u32[]{:S(2)}, u32[]{:S(2)}) collective-permute-start(bf16[3,224,128]{2,1,0:T(8,128)(2,1)S(1)} %get-tuple-element.52), channel_id=1, source_target_pairs={{0,64},{64,128},{128,192},{192,0},{1,65},{65,129},{129,193},{193,1... | collective-permute-start | bytes 516104 | tf_op jit(solution)/shard_map/ppermute | solution.py:39
  125.4 10.6 %collective-permute-start.8 = (bf16[2,3,224,128]{3,2,1,0:T(8,128)(2,1)S(1)}, bf16[2,3,224,128]{3,2,1,0:T(8,128)(2,1)S(1)}, u32[]{:S(2)}, u32[]{:S(2)}) collective-permute-start(bf16[2,3,224,128]{3,2,1,0:T(8,128)(2,1)S(1)} %slice.120), channel_id=1, source_target_pairs={{0,16},{16,32},{32,48},{48,0},{1,17},{17,33},{33,49},{49,1},{2,18}... | collective-permute-start | bytes 1032200 | tf_op jit(solution)/shard_map/ppermute | solution.py:39
  125.9 10.1 %collective-permute-start.9 = (bf16[2,3,224,128]{3,2,1,0:T(8,128)(2,1)S(1)}, bf16[2,3,224,128]{3,2,1,0:T(8,128)(2,1)S(1)}, u32[]{:S(2)}, u32[]{:S(2)}) collective-permute-start(bf16[2,3,224,128]{3,2,1,0:T(8,128)(2,1)S(1)} %slice.121), channel_id=1, source_target_pairs={{0,48},{16,0},{32,16},{48,32},{1,49},{17,1},{33,17},{49,33},{2,50}... | collective-permute-start | bytes 1032200 | tf_op jit(solution)/shard_map/ppermute | solution.py:39
  128.5 10.6 %collective-permute-start.19 = (bf16[3,224,128]{2,1,0:T(8,128)(2,1)S(1)}, bf16[3,224,128]{2,1,0:T(8,128)(2,1)S(1)}, u32[]{:S(2)}, u32[]{:S(2)}) collective-permute-start(bf16[3,224,128]{2,1,0:T(8,128)(2,1)S(1)} %get-tuple-element.72), channel_id=1, source_target_pairs={{0,192},{64,0},{128,64},{192,128},{1,193},{65,1},{129,65},{193,129... | collective-permute-start | bytes 516104 | tf_op jit(solution)/shard_map/ppermute | solution.py:39
  128.6 14.0 %collective-permute-start.18 = (bf16[3,224,128]{2,1,0:T(8,128)(2,1)S(1)}, bf16[3,224,128]{2,1,0:T(8,128)(2,1)S(1)}, u32[]{:S(2)}, u32[]{:S(2)}) collective-permute-start(bf16[3,224,128]{2,1,0:T(8,128)(2,1)S(1)} %get-tuple-element.72), channel_id=1, source_target_pairs={{0,128},{64,192},{128,0},{192,64},{1,129},{65,193},{129,1},{193,65... | collective-permute-start | bytes 516104 | tf_op jit(solution)/shard_map/ppermute | solution.py:39
  128.9 16.2 %collective-permute-start.17 = (bf16[3,224,128]{2,1,0:T(8,128)(2,1)S(1)}, bf16[3,224,128]{2,1,0:T(8,128)(2,1)S(1)}, u32[]{:S(2)}, u32[]{:S(2)}) collective-permute-start(bf16[3,224,128]{2,1,0:T(8,128)(2,1)S(1)} %get-tuple-element.72), channel_id=1, source_target_pairs={{0,64},{64,128},{128,192},{192,0},{1,65},{65,129},{129,193},{193,1... | collective-permute-start | bytes 516104 | tf_op jit(solution)/shard_map/ppermute | solution.py:39
  137.7 10.2 %collective-permute-start.10 = (f32[4,2,2,32,256]{4,3,2,1,0:T(8,128)S(1)}, f32[4,2,2,32,256]{4,3,2,1,0:T(8,128)S(1)}, u32[]{:S(2)}, u32[]{:S(2)}) collective-permute-start(f32[4,2,2,32,256]{4,3,2,1,0:T(8,128)S(1)} %get-tuple-element.35), channel_id=1, source_target_pairs={{0,1},{1,0},{2,3},{3,2},{4,5},{5,4},{6,7},{7,6},{8,9},{9,8},{10,11... | collective-permute-start | bytes 1572872 | tf_op jit(solution)/shard_map/ppermute | solution.py:51
  145.2 17.8 %collective-permute-start.20 = (bf16[4,3,224,128]{3,2,1,0:T(8,128)(2,1)S(1)}, bf16[4,3,224,128]{3,2,1,0:T(8,128)(2,1)S(1)}, u32[]{:S(2)}, u32[]{:S(2)}) collective-permute-start(bf16[4,3,224,128]{3,2,1,0:T(8,128)(2,1)S(1)} %pad_maximum_fusion.1.r0.refs_7_), channel_id=1, source_target_pairs={{0,16},{16,32},{32,48},{48,0},{1,17},{17,33},{33,49},{49,1},{2,18}... | collective-permute-start | bytes 2064392 | tf_op jit(solution)/shard_map/ppermute | solution.py:39
  145.3 17.8 %collective-permute-start.21 = (bf16[4,3,224,128]{3,2,1,0:T(8,128)(2,1)S(1)}, bf16[4,3,224,128]{3,2,1,0:T(8,128)(2,1)S(1)}, u32[]{:S(2)}, u32[]{:S(2)}) collective-permute-start(bf16[4,3,224,128]{3,2,1,0:T(8,128)(2,1)S(1)} %pad_maximum_fusion.1.r0.refs_7_), channel_id=1, source_target_pairs={{0,48},{16,0},{32,16},{48,32},{1,49},{17,1},{33,17},{49,33},{2,50}... | collective-permute-start | bytes 2064392 | tf_op jit(solution)/shard_map/ppermute | solution.py:39
  148.1 17.8 %collective-permute-start.13 = (f32[2,2,32,256]{3,2,1,0:T(8,128)S(1)}, f32[2,2,32,256]{3,2,1,0:T(8,128)S(1)}, u32[]{:S(2)}, u32[]{:S(2)}) collective-permute-start(f32[2,2,32,256]{3,2,1,0:T(8,128)S(1)} %get-tuple-element.59), channel_id=1, source_target_pairs={{0,6},{2,0},{4,2},{6,4},{1,7},{3,1},{5,3},{7,5},{8,14},{10,8},{12,... | collective-permute-start | bytes 393224 | tf_op jit(solution)/shard_map/ppermute | solution.py:39
  149.7 16.2 %collective-permute-start.12 = (f32[2,2,32,256]{3,2,1,0:T(8,128)S(1)}, f32[2,2,32,256]{3,2,1,0:T(8,128)S(1)}, u32[]{:S(2)}, u32[]{:S(2)}) collective-permute-start(f32[2,2,32,256]{3,2,1,0:T(8,128)S(1)} %get-tuple-element.60), channel_id=1, source_target_pairs={{0,4},{2,6},{4,0},{6,2},{1,5},{3,7},{5,1},{7,3},{8,12},{10,14},{12... | collective-permute-start | bytes 393224 | tf_op jit(solution)/shard_map/ppermute | solution.py:39
  150.8 15.1 %collective-permute-start.11 = (f32[2,2,32,256]{3,2,1,0:T(8,128)S(1)}, f32[2,2,32,256]{3,2,1,0:T(8,128)S(1)}, u32[]{:S(2)}, u32[]{:S(2)}) collective-permute-start(f32[2,2,32,256]{3,2,1,0:T(8,128)S(1)} %get-tuple-element.58), channel_id=1, source_target_pairs={{0,2},{2,4},{4,6},{6,0},{1,3},{3,5},{5,7},{7,1},{8,10},{10,12},{12... | collective-permute-start | bytes 393224 | tf_op jit(solution)/shard_map/ppermute | solution.py:39
  163.1 9.5 %collective-permute-start.22 = (bf16[2,3,224,128]{3,2,1,0:T(8,128)(2,1)S(1)}, bf16[2,3,224,128]{3,2,1,0:T(8,128)(2,1)S(1)}, u32[]{:S(2)}, u32[]{:S(2)}) collective-permute-start(bf16[2,3,224,128]{3,2,1,0:T(8,128)(2,1)S(1)} %slice.129), channel_id=1, source_target_pairs={{0,16},{16,32},{32,48},{48,0},{1,17},{17,33},{33,49},{49,1},{2,18}... | collective-permute-start | bytes 1032200 | tf_op jit(solution)/shard_map/ppermute | solution.py:39
  163.2 9.4 %collective-permute-start.23 = (bf16[2,3,224,128]{3,2,1,0:T(8,128)(2,1)S(1)}, bf16[2,3,224,128]{3,2,1,0:T(8,128)(2,1)S(1)}, u32[]{:S(2)}, u32[]{:S(2)}) collective-permute-start(bf16[2,3,224,128]{3,2,1,0:T(8,128)(2,1)S(1)} %slice.130), channel_id=1, source_target_pairs={{0,48},{16,0},{32,16},{48,32},{1,49},{17,1},{33,17},{49,33},{2,50}... | collective-permute-start | bytes 1032200 | tf_op jit(solution)/shard_map/ppermute | solution.py:39
  175.1 3.9 %collective-permute-start.24 = (f32[4,2,2,32,256]{4,3,2,1,0:T(8,128)S(1)}, f32[4,2,2,32,256]{4,3,2,1,0:T(8,128)S(1)}, u32[]{:S(2)}, u32[]{:S(2)}) collective-permute-start(f32[4,2,2,32,256]{4,3,2,1,0:T(8,128)S(1)} %get-tuple-element.39), channel_id=1, source_target_pairs={{0,1},{1,0},{2,3},{3,2},{4,5},{5,4},{6,7},{7,6},{8,9},{9,8},{10,11... | collective-permute-start | bytes 1572872 | tf_op jit(solution)/shard_map/ppermute | solution.py:51
  179.1 10.4 %collective-permute-start.27 = (f32[2,2,32,256]{3,2,1,0:T(8,128)S(1)}, f32[2,2,32,256]{3,2,1,0:T(8,128)S(1)}, u32[]{:S(2)}, u32[]{:S(2)}) collective-permute-start(f32[2,2,32,256]{3,2,1,0:T(8,128)S(1)} %get-tuple-element.56), channel_id=1, source_target_pairs={{0,6},{2,0},{4,2},{6,4},{1,7},{3,1},{5,3},{7,5},{8,14},{10,8},{12,... | collective-permute-start | bytes 393224 | tf_op jit(solution)/shard_map/ppermute | solution.py:39
  181.0 8.5 %collective-permute-start.26 = (f32[2,2,32,256]{3,2,1,0:T(8,128)S(1)}, f32[2,2,32,256]{3,2,1,0:T(8,128)S(1)}, u32[]{:S(2)}, u32[]{:S(2)}) collective-permute-start(f32[2,2,32,256]{3,2,1,0:T(8,128)S(1)} %get-tuple-element.57), channel_id=1, source_target_pairs={{0,4},{2,6},{4,0},{6,2},{1,5},{3,7},{5,1},{7,3},{8,12},{10,14},{12... | collective-permute-start | bytes 393224 | tf_op jit(solution)/shard_map/ppermute | solution.py:39
  182.1 7.4 %collective-permute-start.25 = (f32[2,2,32,256]{3,2,1,0:T(8,128)S(1)}, f32[2,2,32,256]{3,2,1,0:T(8,128)S(1)}, u32[]{:S(2)}, u32[]{:S(2)}) collective-permute-start(f32[2,2,32,256]{3,2,1,0:T(8,128)S(1)} %get-tuple-element.55), channel_id=1, source_target_pairs={{0,2},{2,4},{4,6},{6,0},{1,3},{3,5},{5,7},{7,1},{8,10},{10,12},{12... | collective-permute-start | bytes 393224 | tf_op jit(solution)/shard_map/ppermute | solution.py:39
  189.6 11.3 %collective-permute-start.29 = (bf16[2,64,256]{2,1,0:T(8,128)(2,1)S(1)}, bf16[2,64,256]{2,1,0:T(8,128)(2,1)S(1)}, u32[]{:S(2)}, u32[]{:S(2)}) collective-permute-start(bf16[2,64,256]{2,1,0:T(8,128)(2,1)S(1)} %get-tuple-element.74), channel_id=1, source_target_pairs={{0,128},{1,144},{2,160},{3,176},{4,192},{5,208},{6,224},{7,240},{8... | collective-permute-start | bytes 196616 | tf_op jit(solution)/shard_map/ppermute | solution.py:327
  199.0 10.7 %collective-permute-start.28 = (bf16[2,64,256]{2,1,0:T(8,128)(2,1)S(1)}, bf16[2,64,256]{2,1,0:T(8,128)(2,1)S(1)}, u32[]{:S(2)}, u32[]{:S(2)}) collective-permute-start(bf16[2,64,256]{2,1,0:T(8,128)(2,1)S(1)} %get-tuple-element.73), channel_id=1, source_target_pairs={{0,0},{1,16},{2,32},{3,48},{4,64},{5,80},{6,96},{7,112},{8,128},{9... | collective-permute-start | bytes 196616 | tf_op jit(solution)/shard_map/ppermute | solution.py:327
Sparse Core Ops, SparseCore 0:
  37.2 26.8 all-gather.4
  66.6 28.3 all-gather.6

commit v4 on v3

--- a/solution.py
+++ b/solution.py
@@ -70,33 +70,38 @@
     )(*inputs)
 
 
-def pick_kernel(q_ref, dispatch_ref, weight_ref, tokens_ref, cotangent_ref, out_ref):
-    routed = jnp.dot(dispatch_ref[...], tokens_ref[...], preferred_element_type=F32)
-    grads = jnp.dot(dispatch_ref[...], cotangent_ref[...], preferred_element_type=F32)
-    routed = routed.astype(BF16)
-    grads = (weight_ref[...] * grads).astype(BF16)
-    for y in range(4):
-        out_ref[0, y, 0] = routed
-        out_ref[0, y, 1] = grads
+def pick_kernel(q_ref, dispatch_ref, weight_ref, tokens_ref, cotangent_ref, out_ref, held, sems):
+    q = q_ref[0]
+    copies = []
+    for z in range(4):
+        for t, ref in enumerate((tokens_ref, cotangent_ref)):
+            start = pl.multiple_of((z * 8 + q) * 128, 128)
+            columns = ref.at[:, pl.ds(start, 128)]
+            copies.append(pltpu.make_async_copy(columns, held.at[z, t], sems.at[z, t]))
+            copies[-1].start()
+    for z in range(4):
+        copies[2 * z].wait()
+        copies[2 * z + 1].wait()
+        routed = jnp.dot(dispatch_ref[...], held[z, 0], preferred_element_type=F32)
+        grads = jnp.dot(dispatch_ref[...], held[z, 1], preferred_element_type=F32)
+        routed = routed.astype(BF16)
+        grads = (weight_ref[...] * grads).astype(BF16)
+        for y in range(4):
+            out_ref[z, y, 0] = routed
+            out_ref[z, y, 1] = grads
 
 
 def pick_rows(q, dispatch, weight, tokens, cotangent):
     rows, count = dispatch.shape
     return pl.pallas_call(
         pick_kernel,
-        grid_spec=pltpu.PrefetchScalarGridSpec(
-            num_scalar_prefetch=1,
-            grid=(4,),
-            in_specs=[
-                pl.BlockSpec((rows, count), lambda z, q: (0, 0)),
-                pl.BlockSpec((rows, 1), lambda z, q: (0, 0)),
-                pl.BlockSpec((count, 128), lambda z, q: (0, z * 8 + q[0])),
-                pl.BlockSpec((count, 128), lambda z, q: (0, z * 8 + q[0])),
-            ],
-            out_specs=pl.BlockSpec((1, 4, 2, rows, 128), lambda z, q: (z, 0, 0, 0, 0)),
-        ),
+        in_specs=[pl.BlockSpec(memory_space=pltpu.SMEM)]
+        + [pl.BlockSpec(memory_space=pltpu.VMEM)] * 2
+        + [pl.BlockSpec(memory_space=pltpu.HBM)] * 2,
+        out_specs=pl.BlockSpec(memory_space=pltpu.VMEM),
         out_shape=jax.ShapeDtypeStruct((4, 4, 2, rows, 128), BF16),
-        compiler_params=VMEM,
+        scratch_shapes=[pltpu.VMEM((4, 2, count, 128), BF16), pltpu.SemaphoreType.DMA((4, 2))],
+        compiler_params=pltpu.CompilerParams(vmem_limit_bytes=61 * 2**20),
     )(q, dispatch, weight, tokens, cotangent)
 
 

time: 219 us -> 219 us (level)
    unnamed x16 -> x12, local copies, waits for them, and re-layouts: 8.15 us -> 5.71 us
where the time goes in v4:
time: 219 us; the launch traced here: 218 us
  waiting for transfers between devices  92.9 us (42%)
  starting transfers between devices  55.1 us (25%)
  Pallas kernels  21.3 us (10%)
  blocking collectives  20.5 us (9%)
  between operations  14.4 us (7%)
  local copies, waits for them, and re-layouts  8.69 us (4%)
  other arithmetic  3.63 us (2%)
    ppermute x26, waiting for transfers between devices, shift(): return lax.ppermute(values, axis, [(i, (i + step) % 4) for i in range(4)])  63.3 us
    ppermute x26, starting transfers between devices, shift(): return lax.ppermute(values, axis, [(i, (i + step) % 4) for i in range(4)])  28.7 us
    all_to_all x1, blocking collectives, exchange(): return lax.all_to_all(values, axes, split_axis=0, concat_axis=0, tiled=True)  20.5 us
    all_to_all x2, starting transfers between devices, exchange(): return lax.all_to_all(values, axes, split_axis=0, concat_axis=0, tiled=True)  11.2 us
    all_to_all x2, waiting for transfers between devices, exchange(): return lax.all_to_all(values, axes, split_axis=0, concat_axis=0, tiled=True)  11.2 us
    ppermute x1, starting transfers between devices, local(): lax.ppermute(sums[1], ALL, home_other)  9.46 us
    ppermute x1, waiting for transfers between devices, local(): lax.ppermute(sums[0], ALL, home_same)  8.79 us
    all_gather x2, waiting for transfers between devices, local(): lax.all_gather(sent[:, :, k * CAP:(k + 1) * CAP], ('x', 'c'), axis=0)  7.37 us
  transfers between devices with their start and end apart: 34, of which 18 were waited for; matrix products, arithmetic and copies ran while one was open for 0% of the time, Pallas kernels for 7%

profile of v4, /device:TPU:67, one launch (start us, length us, event | category | flops | bytes accessed | tf_op | source)
XLA Modules:
  0.0 218.4 jit_solution(16268028823448170380)
XLA Ops:
  7.2 0.7 convert_reduce_fusion
  7.9 0.3 reduce_window_sum.11
  8.4 0.7 convert_convert_fusion.dispatch_ref
  9.1 0.7 broadcast_in_dim_reshape.5.weight_ref
  9.8 3.1 %shard_map.111 = bf16[4,4,2,64,128]{4,3,2,1,0:T(8,128)(2,1)} custom-call(s32[1]{0:T(128)} %bitcast.6.q_ref, bf16[64,128]{1,0:T(8,128)(2,1)} %convert_convert_fusion.dispatch_ref, f32[64,1]{1,0:T(8,128)} %broadcast_in_dim_reshape.5.weight_ref, bf16[128,4096]{1,0:T(8,128)(2,1)} %tokens_ref.1, bf16[128,4096]{1,0:T(8,128)(2,1)} %cotangent_ref.1), custom_call_target="tpu_custom_call" | custom-call | tf_op jit(solution)/shard_map/pallas_call | solution.py:96
  12.9 7.7 %all-to-all-start = ((bf16[16,2,64,128]{3,2,1,0:T(8,128)(2,1)}), bf16[16,2,64,128]{3,2,1,0:T(8,128)(2,1)}, u32[]{:S(2)}, u32[]{:S(2)}) async-start(bf16[16,2,64,128]{3,2,1,0:T(8,128)(2,1)} %bitcast.87), calls=%async_computation | async-start | bytes 1048576 | tf_op jit(solution)/shard_map/all_to_all | solution.py:35
  20.7 1.2 copy-done.5
  21.9 2.2 shard_map.110
  24.1 11.2 %all-to-all-done = bf16[16,2,64,128]{3,2,1,0:T(8,128)(2,1)} async-done(((bf16[16,2,64,128]{3,2,1,0:T(8,128)(2,1)}), bf16[16,2,64,128]{3,2,1,0:T(8,128)(2,1)}, u32[]{:S(2)}, u32[]{:S(2)}) %all-to-all-start) | async-done | bytes 524320 | tf_op jit(solution)/shard_map/all_to_all | solution.py:35
  35.3 1.9 fusion.13
  37.2 0.7 all-gather.7.cloned.1.call-update
  37.9 20.5 %all_to_all.15.w_ref = bf16[4,3,224,256]{3,2,1,0:T(8,128)(2,1)} all-to-all(bf16[4,3,224,256]{3,2,1,0:T(8,128)(2,1)S(1)} %get-tuple-element.26.w_ref), channel_id=1, replica_groups=mesh['zl'=4,'y'=4,'zh'=2,'x'=4,'c'=2] {'y'}, dimensions={0} | all-to-all | bytes 2752512 | tf_op jit(solution)/shard_map/all_to_all | solution.py:35
  58.4 3.5 %all-to-all-start.2 = ((bf16[4,3,224,256]{3,2,1,0:T(8,128)(2,1)}), bf16[4,3,224,256]{3,2,1,0:T(8,128)(2,1)S(1)}, u32[]{:S(2)}, u32[]{:S(2)}) async-start(bf16[4,3,224,256]{3,2,1,0:T(8,128)(2,1)} %get-tuple-element.27.w_ref), calls=%async_computation.2 | async-start | bytes 2752512 | tf_op jit(solution)/shard_map/all_to_all | solution.py:35
  62.0 2.2 %all-gather.5.cloned.1.call-done = bf16[128,2,32,128]{3,2,1,0:T(8,128)(2,1)} async-done(((bf16[16,2,32,128]{3,2,1,0:T(8,128)(2,1)}), bf16[128,2,32,128]{3,2,1,0:T(8,128)(2,1)}) %all-gather.5.cloned.1.call-update) | async-done | bytes 2097168 | tf_op jit(solution)/shard_map/all_gather | solution.py:296
  64.2 1.6 copy-done
  65.8 1.3 copy-done.2
  67.1 2.8 %shard_map.112 = (bf16[4,3,224,128]{3,2,1,0:T(8,128)(2,1)S(1)}, f32[3,224,128]{2,1,0:T(8,128)S(1)}) custom-call(s32[5]{0:T(128)S(1)} %stack.65.where_ref, bf16[8,16,2,32,128]{4,3,2,1,0:T(8,128)(2,1)S(1)} %bitcast.84, bf16[4,3,224,256]{3,2,1,0:T(8,128)(2,1)S(1)} %copy-done.2), custom_call_target="tpu_custom_call" | custom-call | flops 704643072 | bytes 6914048 | tf_op jit(solution)/shard_map/pallas_call | solution.py:158
  69.9 0.3 collective-permute-start.2
  70.2 3.2 %collective-permute-start.1 = (bf16[3,224,128]{2,1,0:T(8,128)(2,1)S(1)}, bf16[3,224,128]{2,1,0:T(8,128)(2,1)S(1)}, u32[]{:S(2)}, u32[]{:S(2)}) collective-permute-start(bf16[3,224,128]{2,1,0:T(8,128)(2,1)S(1)} %get-tuple-element.51), channel_id=1, source_target_pairs={{0,128},{64,192},{128,0},{192,64},{1,129},{65,193},{129,1},{193,65... | collective-permute-start | bytes 516104 | tf_op jit(solution)/shard_map/ppermute | solution.py:39
  73.4 2.4 %collective-permute-done.2 = bf16[3,224,128]{2,1,0:T(8,128)(2,1)S(1)} collective-permute-done((bf16[3,224,128]{2,1,0:T(8,128)(2,1)S(1)}, bf16[3,224,128]{2,1,0:T(8,128)(2,1)S(1)}, u32[]{:S(2)}, u32[]{:S(2)}) %collective-permute-start.2) | collective-permute-done | bytes 172064 | tf_op jit(solution)/shard_map/ppermute | solution.py:39
  75.7 9.3 %collective-permute-done.1 = bf16[3,224,128]{2,1,0:T(8,128)(2,1)S(1)} collective-permute-done((bf16[3,224,128]{2,1,0:T(8,128)(2,1)S(1)}, bf16[3,224,128]{2,1,0:T(8,128)(2,1)S(1)}, u32[]{:S(2)}, u32[]{:S(2)}) %collective-permute-start.1) | collective-permute-done | bytes 172064 | tf_op jit(solution)/shard_map/ppermute | solution.py:39
  85.0 3.0 %collective-permute-done = bf16[3,224,128]{2,1,0:T(8,128)(2,1)S(1)} collective-permute-done((bf16[3,224,128]{2,1,0:T(8,128)(2,1)S(1)}, bf16[3,224,128]{2,1,0:T(8,128)(2,1)S(1)}, u32[]{:S(2)}, u32[]{:S(2)}) %collective-permute-start) | collective-permute-done | bytes 172064 | tf_op jit(solution)/shard_map/ppermute | solution.py:39
  88.5 1.4 collective-permute-start.3
  89.9 5.2 %all-gather.7.cloned.1.call-done = bf16[128,2,32,128]{3,2,1,0:T(8,128)(2,1)} async-done(((bf16[16,2,32,128]{3,2,1,0:T(8,128)(2,1)}), bf16[128,2,32,128]{3,2,1,0:T(8,128)(2,1)}) %all-gather.7.cloned.1.call-update) | async-done | bytes 2097168 | tf_op jit(solution)/shard_map/all_gather | solution.py:296
  95.0 1.6 copy-done.1
  96.6 2.8 %shard_map.113 = (bf16[4,3,224,128]{3,2,1,0:T(8,128)(2,1)S(1)}, f32[3,224,128]{2,1,0:T(8,128)S(1)}) custom-call(s32[5]{0:T(128)S(1)} %stack.65.where_ref, bf16[8,16,2,32,128]{4,3,2,1,0:T(8,128)(2,1)S(1)} %bitcast.86, bf16[4,3,224,256]{3,2,1,0:T(8,128)(2,1)S(1)} %all-to-all-done.2.w_ref), custom_call_target="tpu_custom_call" | custom-call | flops 704643072 | bytes 6914048 | tf_op jit(solution)/shard_map/pallas_call | solution.py:158
  99.4 2.8 %collective-permute-done.4 = bf16[3,224,128]{2,1,0:T(8,128)(2,1)S(1)} collective-permute-done((bf16[3,224,128]{2,1,0:T(8,128)(2,1)S(1)}, bf16[3,224,128]{2,1,0:T(8,128)(2,1)S(1)}, u32[]{:S(2)}, u32[]{:S(2)}) %collective-permute-start.4) | collective-permute-done | bytes 172064 | tf_op jit(solution)/shard_map/ppermute | solution.py:39
  102.2 2.2 collective-permute-done.3
  104.4 1.0 pad_maximum_fusion.r0.refs_2_
  105.4 1.5 collective-permute-start.6
  106.9 1.2 collective-permute-start.7
  108.3 1.0 collective-permute-start.15
  109.3 1.4 collective-permute-start.14
  110.7 2.4 %collective-permute-done.16 = bf16[3,224,128]{2,1,0:T(8,128)(2,1)S(1)} collective-permute-done((bf16[3,224,128]{2,1,0:T(8,128)(2,1)S(1)}, bf16[3,224,128]{2,1,0:T(8,128)(2,1)S(1)}, u32[]{:S(2)}, u32[]{:S(2)}) %collective-permute-start.16) | collective-permute-done | bytes 172064 | tf_op jit(solution)/shard_map/ppermute | solution.py:39
  113.1 9.2 %collective-permute-done.15 = bf16[3,224,128]{2,1,0:T(8,128)(2,1)S(1)} collective-permute-done((bf16[3,224,128]{2,1,0:T(8,128)(2,1)S(1)}, bf16[3,224,128]{2,1,0:T(8,128)(2,1)S(1)}, u32[]{:S(2)}, u32[]{:S(2)}) %collective-permute-start.15) | collective-permute-done | bytes 172064 | tf_op jit(solution)/shard_map/ppermute | solution.py:39
  122.3 2.8 %collective-permute-done.14 = bf16[3,224,128]{2,1,0:T(8,128)(2,1)S(1)} collective-permute-done((bf16[3,224,128]{2,1,0:T(8,128)(2,1)S(1)}, bf16[3,224,128]{2,1,0:T(8,128)(2,1)S(1)}, u32[]{:S(2)}, u32[]{:S(2)}) %collective-permute-start.14) | collective-permute-done | bytes 172064 | tf_op jit(solution)/shard_map/ppermute | solution.py:39
  125.2 0.5 collective-permute-start.8
  125.8 2.5 %collective-permute-start.9 = (bf16[2,3,224,128]{3,2,1,0:T(8,128)(2,1)S(1)}, bf16[2,3,224,128]{3,2,1,0:T(8,128)(2,1)S(1)}, u32[]{:S(2)}, u32[]{:S(2)}) collective-permute-start(bf16[2,3,224,128]{3,2,1,0:T(8,128)(2,1)S(1)} %slice.121), channel_id=1, source_target_pairs={{0,48},{16,0},{32,16},{48,32},{1,49},{17,1},{33,17},{49,33},{2,50}... | collective-permute-start | bytes 1032200 | tf_op jit(solution)/shard_map/ppermute | solution.py:39
  128.5 0.4 collective-permute-start.18
  128.8 1.4 collective-permute-start.17
  130.2 5.6 %collective-permute-done.8.r3.refs_5_ = bf16[2,3,224,128]{3,2,1,0:T(8,128)(2,1)S(1)} collective-permute-done((bf16[2,3,224,128]{3,2,1,0:T(8,128)(2,1)S(1)}, bf16[2,3,224,128]{3,2,1,0:T(8,128)(2,1)S(1)}, u32[]{:S(2)}, u32[]{:S(2)}) %collective-permute-start.8) | collective-permute-done | bytes 344096 | tf_op jit(solution)/shard_map/ppermute | solution.py:39
  135.8 1.7 shard_map.114
  137.6 1.4 collective-permute-start.10
  139.0 3.5 %collective-permute-done.18 = bf16[3,224,128]{2,1,0:T(8,128)(2,1)S(1)} collective-permute-done((bf16[3,224,128]{2,1,0:T(8,128)(2,1)S(1)}, bf16[3,224,128]{2,1,0:T(8,128)(2,1)S(1)}, u32[]{:S(2)}, u32[]{:S(2)}) %collective-permute-start.18) | collective-permute-done | bytes 172064 | tf_op jit(solution)/shard_map/ppermute | solution.py:39
  142.5 2.5 %collective-permute-done.17 = bf16[3,224,128]{2,1,0:T(8,128)(2,1)S(1)} collective-permute-done((bf16[3,224,128]{2,1,0:T(8,128)(2,1)S(1)}, bf16[3,224,128]{2,1,0:T(8,128)(2,1)S(1)}, u32[]{:S(2)}, u32[]{:S(2)}) %collective-permute-start.17) | collective-permute-done | bytes 172064 | tf_op jit(solution)/shard_map/ppermute | solution.py:39
  145.2 2.7 %collective-permute-start.21 = (bf16[4,3,224,128]{3,2,1,0:T(8,128)(2,1)S(1)}, bf16[4,3,224,128]{3,2,1,0:T(8,128)(2,1)S(1)}, u32[]{:S(2)}, u32[]{:S(2)}) collective-permute-start(bf16[4,3,224,128]{3,2,1,0:T(8,128)(2,1)S(1)} %pad_maximum_fusion.1.r0.refs_7_), channel_id=1, source_target_pairs={{0,48},{16,0},{32,16},{48,32},{1,49},{17,1},{33,17},{49,33},{2,50}... | collective-permute-start | bytes 2064392 | tf_op jit(solution)/shard_map/ppermute | solution.py:39
  147.9 1.6 collective-permute-start.13
  149.6 1.1 collective-permute-start.12
  150.7 1.2 collective-permute-start.11
  151.8 11.0 %collective-permute-done.20.r1.refs_8_ = bf16[4,3,224,128]{3,2,1,0:T(8,128)(2,1)S(1)} collective-permute-done((bf16[4,3,224,128]{3,2,1,0:T(8,128)(2,1)S(1)}, bf16[4,3,224,128]{3,2,1,0:T(8,128)(2,1)S(1)}, u32[]{:S(2)}, u32[]{:S(2)}) %collective-permute-start.20) | collective-permute-done | bytes 688160 | tf_op jit(solution)/shard_map/ppermute | solution.py:39
  163.0 2.7 %collective-permute-start.23 = (bf16[2,3,224,128]{3,2,1,0:T(8,128)(2,1)S(1)}, bf16[2,3,224,128]{3,2,1,0:T(8,128)(2,1)S(1)}, u32[]{:S(2)}, u32[]{:S(2)}) collective-permute-start(bf16[2,3,224,128]{3,2,1,0:T(8,128)(2,1)S(1)} %slice.130), channel_id=1, source_target_pairs={{0,48},{16,0},{32,16},{48,32},{1,49},{17,1},{33,17},{49,33},{2,50}... | collective-permute-start | bytes 1032200 | tf_op jit(solution)/shard_map/ppermute | solution.py:39
  165.8 6.6 %collective-permute-done.22.r3.refs_10_ = bf16[2,3,224,128]{3,2,1,0:T(8,128)(2,1)S(1)} collective-permute-done((bf16[2,3,224,128]{3,2,1,0:T(8,128)(2,1)S(1)}, bf16[2,3,224,128]{3,2,1,0:T(8,128)(2,1)S(1)}, u32[]{:S(2)}, u32[]{:S(2)}) %collective-permute-start.22) | collective-permute-done | bytes 344096 | tf_op jit(solution)/shard_map/ppermute | solution.py:39
  172.4 2.5 %shard_map.115 = (f32[4,2,2,32,256]{4,3,2,1,0:T(8,128)S(1)}, f32[4,2,2,32,256]{4,3,2,1,0:T(8,128)S(1)}) custom-call(s32[5]{0:T(128)S(1)} %stack.65.where_ref, bf16[4,3,224,256]{3,2,1,0:T(8,128)(2,1)} %get-tuple-element.27.w_ref, bf16[4,3,224,128]{3,2,1,0:T(8,128)(2,1)S(1)} %pad_maximum_fusion.1.r0.refs_7_, ...), custom_call_target="tpu_custom_call" | custom-call | flops 704643072 | bytes 5177364 | tf_op jit(solution)/shard_map/pallas_call | solution.py:61
  174.9 2.3 %collective-permute-start.24 = (f32[4,2,2,32,256]{4,3,2,1,0:T(8,128)S(1)}, f32[4,2,2,32,256]{4,3,2,1,0:T(8,128)S(1)}, u32[]{:S(2)}, u32[]{:S(2)}) collective-permute-start(f32[4,2,2,32,256]{4,3,2,1,0:T(8,128)S(1)} %get-tuple-element.39), channel_id=1, source_target_pairs={{0,1},{1,0},{2,3},{3,2},{4,5},{5,4},{6,7},{7,6},{8,9},{9,8},{10,11... | collective-permute-start | bytes 1572872 | tf_op jit(solution)/shard_map/ppermute | solution.py:51
  177.4 1.5 collective-permute-done.24
  178.9 1.8 collective-permute-start.27
  180.8 1.1 collective-permute-start.26
  181.9 1.2 collective-permute-start.25
  183.0 6.3 %shard_map.116 = (f32[2,256,896]{2,1,0:T(8,128)}, f32[2,256,896]{2,1,0:T(8,128)}, f32[2,896,256]{2,1,0:T(8,128)}) custom-call(s32[5]{0:T(128)S(1)} %stack.65.where_ref, bf16[8,16,2,32,128]{4,3,2,1,0:T(8,128)(2,1)} %bitcast.83, bf16[8,16,2,32,128]{4,3,2,1,0:T(8,128)(2,1)} %bitcast.85, bf16[4,3,224,128]{3,2,1,0:T(8,128)(2,1)S(1)} %pad_maximum_fusion.r0.refs_2_, ...), custom_call_target="tpu_custom_call" | custom-call | flops 1409286144 | bytes 12582912 | tf_op jit(solution)/shard_map/pallas_call | solution.py:258
  189.4 9.5 %collective-permute-start.29 = (bf16[2,64,256]{2,1,0:T(8,128)(2,1)S(1)}, bf16[2,64,256]{2,1,0:T(8,128)(2,1)S(1)}, u32[]{:S(2)}, u32[]{:S(2)}) collective-permute-start(bf16[2,64,256]{2,1,0:T(8,128)(2,1)S(1)} %get-tuple-element.74), channel_id=1, source_target_pairs={{0,128},{1,144},{2,160},{3,176},{4,192},{5,208},{6,224},{7,240},{8... | collective-permute-start | bytes 196616 | tf_op jit(solution)/shard_map/ppermute | solution.py:332
  198.9 1.9 collective-permute-start.28
  200.8 8.8 %collective-permute-done.28 = bf16[2,64,256]{2,1,0:T(8,128)(2,1)S(1)} collective-permute-done((bf16[2,64,256]{2,1,0:T(8,128)(2,1)S(1)}, bf16[2,64,256]{2,1,0:T(8,128)(2,1)S(1)}, u32[]{:S(2)}, u32[]{:S(2)}) %collective-permute-start.28) | collective-permute-done | bytes 65568 | tf_op jit(solution)/shard_map/ppermute | solution.py:332
  209.6 1.0 fusion.8
  210.6 0.9 fusion.7
  (65 shorter events, 2.1 us)
Async XLA Ops:
  9.8 10.9 %copy-start.3 = (bf16[2,256,896]{2,1,0:T(8,128)(2,1)S(1)}, bf16[2,256,896]{2,1,0:T(8,128)(2,1)}, u32[]{:S(2)}) copy-start(bf16[2,256,896]{2,1,0:T(8,128)(2,1)} %gate_ref.1) | copy-start | bytes 2752516
  9.8 10.9 %copy-start.4 = (bf16[2,256,896]{2,1,0:T(8,128)(2,1)S(1)}, bf16[2,256,896]{2,1,0:T(8,128)(2,1)}, u32[]{:S(2)}) copy-start(bf16[2,256,896]{2,1,0:T(8,128)(2,1)} %up_ref.1) | copy-start | bytes 2752516
  12.9 22.3 %all-to-all-start = ((bf16[16,2,64,128]{3,2,1,0:T(8,128)(2,1)}), bf16[16,2,64,128]{3,2,1,0:T(8,128)(2,1)}, u32[]{:S(2)}, u32[]{:S(2)}) async-start(bf16[16,2,64,128]{3,2,1,0:T(8,128)(2,1)} %bitcast.87), calls=%async_computation | async-start | bytes 1048576 | tf_op jit(solution)/shard_map/all_to_all | solution.py:35
  20.6 43.6 %all-gather.5.cloned.1.call-start = ((), (), s32[]{:S(2)}) async-start(), calls=%async_computation.3 | async-start | bytes 2359296 | tf_op jit(solution)/shard_map/all_gather | solution.py:296
  20.7 1.2 copy-start.5
  37.1 57.9 %all-gather.7.cloned.1.call-start = ((), (), s32[]{:S(2)}) async-start(), calls=%async_computation.4 | async-start | bytes 2359296 | tf_op jit(solution)/shard_map/all_gather | solution.py:296
  58.4 29.6 %all-to-all-start.2 = ((bf16[4,3,224,256]{3,2,1,0:T(8,128)(2,1)}), bf16[4,3,224,256]{3,2,1,0:T(8,128)(2,1)S(1)}, u32[]{:S(2)}, u32[]{:S(2)}) async-start(bf16[4,3,224,256]{3,2,1,0:T(8,128)(2,1)} %get-tuple-element.27.w_ref), calls=%async_computation.2 | async-start | bytes 2752512 | tf_op jit(solution)/shard_map/all_to_all | solution.py:35
  64.2 1.6 copy-start
  65.8 1.3 copy-start.2
  69.9 5.8 %collective-permute-start.2 = (bf16[3,224,128]{2,1,0:T(8,128)(2,1)S(1)}, bf16[3,224,128]{2,1,0:T(8,128)(2,1)S(1)}, u32[]{:S(2)}, u32[]{:S(2)}) collective-permute-start(bf16[3,224,128]{2,1,0:T(8,128)(2,1)S(1)} %get-tuple-element.50), channel_id=1, source_target_pairs={{0,192},{64,0},{128,64},{192,128},{1,193},{65,1},{129,65},{193,129... | collective-permute-start | bytes 516104 | tf_op jit(solution)/shard_map/ppermute | solution.py:39
  70.2 14.8 %collective-permute-start.1 = (bf16[3,224,128]{2,1,0:T(8,128)(2,1)S(1)}, bf16[3,224,128]{2,1,0:T(8,128)(2,1)S(1)}, u32[]{:S(2)}, u32[]{:S(2)}) collective-permute-start(bf16[3,224,128]{2,1,0:T(8,128)(2,1)S(1)} %get-tuple-element.51), channel_id=1, source_target_pairs={{0,128},{64,192},{128,0},{192,64},{1,129},{65,193},{129,1},{193,65... | collective-permute-start | bytes 516104 | tf_op jit(solution)/shard_map/ppermute | solution.py:39
  73.4 14.6 %collective-permute-start = (bf16[3,224,128]{2,1,0:T(8,128)(2,1)S(1)}, bf16[3,224,128]{2,1,0:T(8,128)(2,1)S(1)}, u32[]{:S(2)}, u32[]{:S(2)}) collective-permute-start(bf16[3,224,128]{2,1,0:T(8,128)(2,1)S(1)} %get-tuple-element.49), channel_id=1, source_target_pairs={{0,64},{64,128},{128,192},{192,0},{1,65},{65,129},{129,193},{193,1... | collective-permute-start | bytes 516104 | tf_op jit(solution)/shard_map/ppermute | solution.py:39
  88.2 11.2 %collective-permute-start.5 = (bf16[3,224,128]{2,1,0:T(8,128)(2,1)S(1)}, bf16[3,224,128]{2,1,0:T(8,128)(2,1)S(1)}, u32[]{:S(2)}, u32[]{:S(2)}) collective-permute-start(bf16[3,224,128]{2,1,0:T(8,128)(2,1)S(1)} %get-tuple-element.70), channel_id=1, source_target_pairs={{0,192},{64,0},{128,64},{192,128},{1,193},{65,1},{129,65},{193,129... | collective-permute-start | bytes 516104 | tf_op jit(solution)/shard_map/ppermute | solution.py:39
  88.3 13.9 %collective-permute-start.4 = (bf16[3,224,128]{2,1,0:T(8,128)(2,1)S(1)}, bf16[3,224,128]{2,1,0:T(8,128)(2,1)S(1)}, u32[]{:S(2)}, u32[]{:S(2)}) collective-permute-start(bf16[3,224,128]{2,1,0:T(8,128)(2,1)S(1)} %get-tuple-element.70), channel_id=1, source_target_pairs={{0,128},{64,192},{128,0},{192,64},{1,129},{65,193},{129,1},{193,65... | collective-permute-start | bytes 516104 | tf_op jit(solution)/shard_map/ppermute | solution.py:39
  88.5 15.9 %collective-permute-start.3 = (bf16[3,224,128]{2,1,0:T(8,128)(2,1)S(1)}, bf16[3,224,128]{2,1,0:T(8,128)(2,1)}, u32[]{:S(2)}, u32[]{:S(2)}) collective-permute-start(bf16[3,224,128]{2,1,0:T(8,128)(2,1)S(1)} %get-tuple-element.70), channel_id=1, source_target_pairs={{0,64},{64,128},{128,192},{192,0},{1,65},{65,129},{129,193},{193,1... | collective-permute-start | bytes 516104 | tf_op jit(solution)/shard_map/ppermute | solution.py:39
  95.0 1.6 copy-start.1
  105.4 19.8 %collective-permute-start.6 = (bf16[4,3,224,128]{3,2,1,0:T(8,128)(2,1)S(1)}, bf16[4,3,224,128]{3,2,1,0:T(8,128)(2,1)S(1)}, u32[]{:S(2)}, u32[]{:S(2)}) collective-permute-start(bf16[4,3,224,128]{3,2,1,0:T(8,128)(2,1)S(1)} %pad_maximum_fusion.r0.refs_2_), channel_id=1, source_target_pairs={{0,16},{16,32},{32,48},{48,0},{1,17},{17,33},{33,49},{49,1},{2,18}... | collective-permute-start | bytes 2064392 | tf_op jit(solution)/shard_map/ppermute | solution.py:39
  106.9 18.8 %collective-permute-start.7 = (bf16[4,3,224,128]{3,2,1,0:T(8,128)(2,1)S(1)}, bf16[4,3,224,128]{3,2,1,0:T(8,128)(2,1)S(1)}, u32[]{:S(2)}, u32[]{:S(2)}) collective-permute-start(bf16[4,3,224,128]{3,2,1,0:T(8,128)(2,1)S(1)} %pad_maximum_fusion.r0.refs_2_), channel_id=1, source_target_pairs={{0,48},{16,0},{32,16},{48,32},{1,49},{17,1},{33,17},{49,33},{2,50}... | collective-permute-start | bytes 2064392 | tf_op jit(solution)/shard_map/ppermute | solution.py:39
  108.2 4.9 %collective-permute-start.16 = (bf16[3,224,128]{2,1,0:T(8,128)(2,1)S(1)}, bf16[3,224,128]{2,1,0:T(8,128)(2,1)S(1)}, u32[]{:S(2)}, u32[]{:S(2)}) collective-permute-start(bf16[3,224,128]{2,1,0:T(8,128)(2,1)S(1)} %get-tuple-element.53), channel_id=1, source_target_pairs={{0,192},{64,0},{128,64},{192,128},{1,193},{65,1},{129,65},{193,129... | collective-permute-start | bytes 516104 | tf_op jit(solution)/shard_map/ppermute | solution.py:39
  108.3 14.0 %collective-permute-start.15 = (bf16[3,224,128]{2,1,0:T(8,128)(2,1)S(1)}, bf16[3,224,128]{2,1,0:T(8,128)(2,1)S(1)}, u32[]{:S(2)}, u32[]{:S(2)}) collective-permute-start(bf16[3,224,128]{2,1,0:T(8,128)(2,1)S(1)} %get-tuple-element.54), channel_id=1, source_target_pairs={{0,128},{64,192},{128,0},{192,64},{1,129},{65,193},{129,1},{193,65... | collective-permute-start | bytes 516104 | tf_op jit(solution)/shard_map/ppermute | solution.py:39
  109.3 15.8 %collective-permute-start.14 = (bf16[3,224,128]{2,1,0:T(8,128)(2,1)S(1)}, bf16[3,224,128]{2,1,0:T(8,128)(2,1)S(1)}, u32[]{:S(2)}, u32[]{:S(2)}) collective-permute-start(bf16[3,224,128]{2,1,0:T(8,128)(2,1)S(1)} %get-tuple-element.52), channel_id=1, source_target_pairs={{0,64},{64,128},{128,192},{192,0},{1,65},{65,129},{129,193},{193,1... | collective-permute-start | bytes 516104 | tf_op jit(solution)/shard_map/ppermute | solution.py:39
  125.2 10.6 %collective-permute-start.8 = (bf16[2,3,224,128]{3,2,1,0:T(8,128)(2,1)S(1)}, bf16[2,3,224,128]{3,2,1,0:T(8,128)(2,1)S(1)}, u32[]{:S(2)}, u32[]{:S(2)}) collective-permute-start(bf16[2,3,224,128]{3,2,1,0:T(8,128)(2,1)S(1)} %slice.120), channel_id=1, source_target_pairs={{0,16},{16,32},{32,48},{48,0},{1,17},{17,33},{33,49},{49,1},{2,18}... | collective-permute-start | bytes 1032200 | tf_op jit(solution)/shard_map/ppermute | solution.py:39
  125.8 10.1 %collective-permute-start.9 = (bf16[2,3,224,128]{3,2,1,0:T(8,128)(2,1)S(1)}, bf16[2,3,224,128]{3,2,1,0:T(8,128)(2,1)S(1)}, u32[]{:S(2)}, u32[]{:S(2)}) collective-permute-start(bf16[2,3,224,128]{3,2,1,0:T(8,128)(2,1)S(1)} %slice.121), channel_id=1, source_target_pairs={{0,48},{16,0},{32,16},{48,32},{1,49},{17,1},{33,17},{49,33},{2,50}... | collective-permute-start | bytes 1032200 | tf_op jit(solution)/shard_map/ppermute | solution.py:39
  128.4 10.6 %collective-permute-start.19 = (bf16[3,224,128]{2,1,0:T(8,128)(2,1)S(1)}, bf16[3,224,128]{2,1,0:T(8,128)(2,1)S(1)}, u32[]{:S(2)}, u32[]{:S(2)}) collective-permute-start(bf16[3,224,128]{2,1,0:T(8,128)(2,1)S(1)} %get-tuple-element.72), channel_id=1, source_target_pairs={{0,192},{64,0},{128,64},{192,128},{1,193},{65,1},{129,65},{193,129... | collective-permute-start | bytes 516104 | tf_op jit(solution)/shard_map/ppermute | solution.py:39
  128.5 14.0 %collective-permute-start.18 = (bf16[3,224,128]{2,1,0:T(8,128)(2,1)S(1)}, bf16[3,224,128]{2,1,0:T(8,128)(2,1)S(1)}, u32[]{:S(2)}, u32[]{:S(2)}) collective-permute-start(bf16[3,224,128]{2,1,0:T(8,128)(2,1)S(1)} %get-tuple-element.72), channel_id=1, source_target_pairs={{0,128},{64,192},{128,0},{192,64},{1,129},{65,193},{129,1},{193,65... | collective-permute-start | bytes 516104 | tf_op jit(solution)/shard_map/ppermute | solution.py:39
  128.8 16.1 %collective-permute-start.17 = (bf16[3,224,128]{2,1,0:T(8,128)(2,1)S(1)}, bf16[3,224,128]{2,1,0:T(8,128)(2,1)S(1)}, u32[]{:S(2)}, u32[]{:S(2)}) collective-permute-start(bf16[3,224,128]{2,1,0:T(8,128)(2,1)S(1)} %get-tuple-element.72), channel_id=1, source_target_pairs={{0,64},{64,128},{128,192},{192,0},{1,65},{65,129},{129,193},{193,1... | collective-permute-start | bytes 516104 | tf_op jit(solution)/shard_map/ppermute | solution.py:39
  137.6 10.3 %collective-permute-start.10 = (f32[4,2,2,32,256]{4,3,2,1,0:T(8,128)S(1)}, f32[4,2,2,32,256]{4,3,2,1,0:T(8,128)S(1)}, u32[]{:S(2)}, u32[]{:S(2)}) collective-permute-start(f32[4,2,2,32,256]{4,3,2,1,0:T(8,128)S(1)} %get-tuple-element.35), channel_id=1, source_target_pairs={{0,1},{1,0},{2,3},{3,2},{4,5},{5,4},{6,7},{7,6},{8,9},{9,8},{10,11... | collective-permute-start | bytes 1572872 | tf_op jit(solution)/shard_map/ppermute | solution.py:51
  145.1 17.8 %collective-permute-start.20 = (bf16[4,3,224,128]{3,2,1,0:T(8,128)(2,1)S(1)}, bf16[4,3,224,128]{3,2,1,0:T(8,128)(2,1)S(1)}, u32[]{:S(2)}, u32[]{:S(2)}) collective-permute-start(bf16[4,3,224,128]{3,2,1,0:T(8,128)(2,1)S(1)} %pad_maximum_fusion.1.r0.refs_7_), channel_id=1, source_target_pairs={{0,16},{16,32},{32,48},{48,0},{1,17},{17,33},{33,49},{49,1},{2,18}... | collective-permute-start | bytes 2064392 | tf_op jit(solution)/shard_map/ppermute | solution.py:39
  145.2 17.8 %collective-permute-start.21 = (bf16[4,3,224,128]{3,2,1,0:T(8,128)(2,1)S(1)}, bf16[4,3,224,128]{3,2,1,0:T(8,128)(2,1)S(1)}, u32[]{:S(2)}, u32[]{:S(2)}) collective-permute-start(bf16[4,3,224,128]{3,2,1,0:T(8,128)(2,1)S(1)} %pad_maximum_fusion.1.r0.refs_7_), channel_id=1, source_target_pairs={{0,48},{16,0},{32,16},{48,32},{1,49},{17,1},{33,17},{49,33},{2,50}... | collective-permute-start | bytes 2064392 | tf_op jit(solution)/shard_map/ppermute | solution.py:39
  147.9 17.8 %collective-permute-start.13 = (f32[2,2,32,256]{3,2,1,0:T(8,128)S(1)}, f32[2,2,32,256]{3,2,1,0:T(8,128)S(1)}, u32[]{:S(2)}, u32[]{:S(2)}) collective-permute-start(f32[2,2,32,256]{3,2,1,0:T(8,128)S(1)} %get-tuple-element.59), channel_id=1, source_target_pairs={{0,6},{2,0},{4,2},{6,4},{1,7},{3,1},{5,3},{7,5},{8,14},{10,8},{12,... | collective-permute-start | bytes 393224 | tf_op jit(solution)/shard_map/ppermute | solution.py:39
  149.6 16.2 %collective-permute-start.12 = (f32[2,2,32,256]{3,2,1,0:T(8,128)S(1)}, f32[2,2,32,256]{3,2,1,0:T(8,128)S(1)}, u32[]{:S(2)}, u32[]{:S(2)}) collective-permute-start(f32[2,2,32,256]{3,2,1,0:T(8,128)S(1)} %get-tuple-element.60), channel_id=1, source_target_pairs={{0,4},{2,6},{4,0},{6,2},{1,5},{3,7},{5,1},{7,3},{8,12},{10,14},{12... | collective-permute-start | bytes 393224 | tf_op jit(solution)/shard_map/ppermute | solution.py:39
  150.7 15.1 %collective-permute-start.11 = (f32[2,2,32,256]{3,2,1,0:T(8,128)S(1)}, f32[2,2,32,256]{3,2,1,0:T(8,128)S(1)}, u32[]{:S(2)}, u32[]{:S(2)}) collective-permute-start(f32[2,2,32,256]{3,2,1,0:T(8,128)S(1)} %get-tuple-element.58), channel_id=1, source_target_pairs={{0,2},{2,4},{4,6},{6,0},{1,3},{3,5},{5,7},{7,1},{8,10},{10,12},{12... | collective-permute-start | bytes 393224 | tf_op jit(solution)/shard_map/ppermute | solution.py:39
  162.9 9.5 %collective-permute-start.22 = (bf16[2,3,224,128]{3,2,1,0:T(8,128)(2,1)S(1)}, bf16[2,3,224,128]{3,2,1,0:T(8,128)(2,1)S(1)}, u32[]{:S(2)}, u32[]{:S(2)}) collective-permute-start(bf16[2,3,224,128]{3,2,1,0:T(8,128)(2,1)S(1)} %slice.129), channel_id=1, source_target_pairs={{0,16},{16,32},{32,48},{48,0},{1,17},{17,33},{33,49},{49,1},{2,18}... | collective-permute-start | bytes 1032200 | tf_op jit(solution)/shard_map/ppermute | solution.py:39
  163.0 9.4 %collective-permute-start.23 = (bf16[2,3,224,128]{3,2,1,0:T(8,128)(2,1)S(1)}, bf16[2,3,224,128]{3,2,1,0:T(8,128)(2,1)S(1)}, u32[]{:S(2)}, u32[]{:S(2)}) collective-permute-start(bf16[2,3,224,128]{3,2,1,0:T(8,128)(2,1)S(1)} %slice.130), channel_id=1, source_target_pairs={{0,48},{16,0},{32,16},{48,32},{1,49},{17,1},{33,17},{49,33},{2,50}... | collective-permute-start | bytes 1032200 | tf_op jit(solution)/shard_map/ppermute | solution.py:39
  174.9 3.9 %collective-permute-start.24 = (f32[4,2,2,32,256]{4,3,2,1,0:T(8,128)S(1)}, f32[4,2,2,32,256]{4,3,2,1,0:T(8,128)S(1)}, u32[]{:S(2)}, u32[]{:S(2)}) collective-permute-start(f32[4,2,2,32,256]{4,3,2,1,0:T(8,128)S(1)} %get-tuple-element.39), channel_id=1, source_target_pairs={{0,1},{1,0},{2,3},{3,2},{4,5},{5,4},{6,7},{7,6},{8,9},{9,8},{10,11... | collective-permute-start | bytes 1572872 | tf_op jit(solution)/shard_map/ppermute | solution.py:51
  178.9 10.4 %collective-permute-start.27 = (f32[2,2,32,256]{3,2,1,0:T(8,128)S(1)}, f32[2,2,32,256]{3,2,1,0:T(8,128)S(1)}, u32[]{:S(2)}, u32[]{:S(2)}) collective-permute-start(f32[2,2,32,256]{3,2,1,0:T(8,128)S(1)} %get-tuple-element.56), channel_id=1, source_target_pairs={{0,6},{2,0},{4,2},{6,4},{1,7},{3,1},{5,3},{7,5},{8,14},{10,8},{12,... | collective-permute-start | bytes 393224 | tf_op jit(solution)/shard_map/ppermute | solution.py:39
  180.8 8.5 %collective-permute-start.26 = (f32[2,2,32,256]{3,2,1,0:T(8,128)S(1)}, f32[2,2,32,256]{3,2,1,0:T(8,128)S(1)}, u32[]{:S(2)}, u32[]{:S(2)}) collective-permute-start(f32[2,2,32,256]{3,2,1,0:T(8,128)S(1)} %get-tuple-element.57), channel_id=1, source_target_pairs={{0,4},{2,6},{4,0},{6,2},{1,5},{3,7},{5,1},{7,3},{8,12},{10,14},{12... | collective-permute-start | bytes 393224 | tf_op jit(solution)/shard_map/ppermute | solution.py:39
  181.9 7.4 %collective-permute-start.25 = (f32[2,2,32,256]{3,2,1,0:T(8,128)S(1)}, f32[2,2,32,256]{3,2,1,0:T(8,128)S(1)}, u32[]{:S(2)}, u32[]{:S(2)}) collective-permute-start(f32[2,2,32,256]{3,2,1,0:T(8,128)S(1)} %get-tuple-element.55), channel_id=1, source_target_pairs={{0,2},{2,4},{4,6},{6,0},{1,3},{3,5},{5,7},{7,1},{8,10},{10,12},{12... | collective-permute-start | bytes 393224 | tf_op jit(solution)/shard_map/ppermute | solution.py:39
  189.4 11.4 %collective-permute-start.29 = (bf16[2,64,256]{2,1,0:T(8,128)(2,1)S(1)}, bf16[2,64,256]{2,1,0:T(8,128)(2,1)S(1)}, u32[]{:S(2)}, u32[]{:S(2)}) collective-permute-start(bf16[2,64,256]{2,1,0:T(8,128)(2,1)S(1)} %get-tuple-element.74), channel_id=1, source_target_pairs={{0,128},{1,144},{2,160},{3,176},{4,192},{5,208},{6,224},{7,240},{8... | collective-permute-start | bytes 196616 | tf_op jit(solution)/shard_map/ppermute | solution.py:332
  198.9 10.7 %collective-permute-start.28 = (bf16[2,64,256]{2,1,0:T(8,128)(2,1)S(1)}, bf16[2,64,256]{2,1,0:T(8,128)(2,1)S(1)}, u32[]{:S(2)}, u32[]{:S(2)}) collective-permute-start(bf16[2,64,256]{2,1,0:T(8,128)(2,1)S(1)} %get-tuple-element.73), channel_id=1, source_target_pairs={{0,0},{1,16},{2,32},{3,48},{4,64},{5,80},{6,96},{7,112},{8,128},{9... | collective-permute-start | bytes 196616 | tf_op jit(solution)/shard_map/ppermute | solution.py:332
Sparse Core Ops, SparseCore 0:
  37.3 26.8 all-gather.4
  66.6 28.3 all-gather.6
